TPU v7x, 512 devices: a whole 4x4x16 slice. The times are simulated.
512 devices in a mesh: ctx: 128 (over z, x, y_hi), head: 4 (over y_lo, core).
Axes of the slice: x: 4, y: 4 (y_hi: 2, y_lo: 2; y = y_hi * 2 + y_lo), z: 16, core: 2. Of those that a mesh axis runs over, the one named last changes fastest.
Arguments:
- fine_q: bfloat16 [16384, 2048], P('ctx', 'head'), may hold values from -19 to 19
- fine_k: bfloat16 [16384, 2048], P('ctx', 'head'), may hold values from -19 to 19
- fine_v: bfloat16 [16384, 2048], P('ctx', 'head'), may hold values from -6 to 6
- fine_x: bfloat16 [16384, 2048], P('ctx', 'head'), may hold values from -6 to 6
- conv_weight: bfloat16 [8, 2048, 4096], P(None, 'head', 'ctx'), may hold values from -0.046875 to 0.046875
- qkv_weight: bfloat16 [128, 256, 3, 512], P('ctx', None, None, 'head'), may hold values from -0.09375 to 0.09375
Outputs:
- fine_out: bfloat16 [16384, 2048], P('ctx', 'head')
- coarse_out: bfloat16 [128, 128, 512], P('ctx', None, 'head')
All inputs are finite; a program needn't handle non-finite values.
Results may differ from a plain program's by a relative error of at most 0.008.
Values may be sent and summed in bfloat16 or wider, within the bound.
A program may use at most 128 MiB of HBM per device.

v0:
```python
import jax
import jax.numpy as jnp
from jax import lax
from jax.sharding import PartitionSpec as P

STRIDE = 8
FINE_STEPS = 2
COARSE_STEPS = 4
HEAD_DIM = 128
HEADS_SUB = 4


def partner_2(block, axis, stride):
    count = lax.axis_size(axis)
    route = []
    for low in range(count):
        high = low | 1 << stride
        if high != low and high < count:
            route += [(low, high), (high, low)]
    return lax.ppermute(block, axis, route)


def passed_along(x, axis, by):
    devices = lax.axis_size(axis)
    pairs = [(i, i + by) for i in range(devices) if 0 <= i + by < devices]
    return lax.ppermute(x, axis, pairs)


def window_valid(row_count, step_count, block_place):
    query_pos = lax.broadcasted_iota(jnp.int32, (row_count, step_count * row_count), 0)
    key_pos = lax.broadcasted_iota(jnp.int32, (row_count, step_count * row_count), 1)
    blocks_back = step_count - 1 - key_pos // row_count
    inner_pos = key_pos % row_count
    return (blocks_back <= block_place) & ((blocks_back > 0) | (inner_pos <= query_pos))


def attend(queries, key_rows, value_rows, key_valid, head_size):
    row_count = queries.shape[0]
    key_count = key_rows.shape[0]
    head_count = queries.shape[1] // head_size
    q_heads = queries.reshape(row_count, head_count, head_size)
    k_heads = key_rows.reshape(key_count, head_count, head_size)
    v_heads = value_rows.reshape(key_count, head_count, head_size)
    scores = jnp.einsum(
        "rhd,shd->hrs", q_heads, k_heads, preferred_element_type=jnp.float32
    ) * head_size ** (-0.5)
    scores = jnp.where(key_valid[None], scores, -1e30)
    row_max = jnp.max(scores, axis=-1, keepdims=True)
    exp_terms = jnp.exp(scores - row_max)
    weights = (exp_terms / jnp.sum(exp_terms, axis=-1, keepdims=True)).astype(jnp.bfloat16)
    mixed_heads = jnp.einsum("hrs,shd->rhd", weights, v_heads, preferred_element_type=jnp.float32)
    return mixed_heads.reshape(row_count, head_count * head_size)


def doubling(local_piece, first_bit, section_count, position, swapper):
    gathered = local_piece[None]
    for section_index in range(section_count):
        bit_index = first_bit + section_index
        partner = swapper(gathered, bit_index)
        upper_half = position >> bit_index & 1 == 1
        gathered = jnp.where(
            upper_half,
            jnp.concatenate([partner, gathered], 0),
            jnp.concatenate([gathered, partner], 0),
        )
    return gathered


def window_keys(own_pair, step_count, shifter):
    earlier = [own_pair]
    for back_index in range(step_count - 1):
        earlier.append(shifter(earlier[-1]))
    ordered = earlier[::-1]
    key_rows = jnp.concatenate([pair_item[0] for pair_item in ordered], 0)
    value_rows = jnp.concatenate([pair_item[1] for pair_item in ordered], 0)
    return (key_rows, value_rows)


def per_device(fine_q, fine_k, fine_v, fine_x, conv_weight, qkv_weight):
    row_count = fine_q.shape[0]
    device_place = lax.axis_index("ctx")
    block_count = lax.axis_size("ctx") // STRIDE
    sub_bits = STRIDE.bit_length() - 1
    block_bits = block_count.bit_length() - 1

    def rows_swapper(gathered, bit_index):
        return partner_2(gathered, "ctx", bit_index)

    def weight_swapper(gathered, bit_index):
        return partner_2(gathered, "ctx", bit_index)

    def fine_shifter(pair_rows):
        return passed_along(pair_rows, "ctx", 1)

    def coarse_shifter(pair_rows):
        return passed_along(pair_rows, "ctx", STRIDE)

    key_rows, value_rows = window_keys(jnp.stack([fine_k, fine_v]), FINE_STEPS, fine_shifter)
    key_valid = window_valid(row_count, FINE_STEPS, device_place)
    fine_mix = attend(fine_q, key_rows, value_rows, key_valid, HEAD_DIM)
    fine_out = (fine_x.astype(jnp.float32) + fine_mix).astype(jnp.bfloat16)
    packed = jnp.concatenate([conv_weight.reshape(-1), qkv_weight.reshape(-1)])
    weight_stack = doubling(packed, sub_bits, block_bits, device_place, weight_swapper)
    feature_count = fine_out.shape[1]
    token_piece = fine_out.reshape(row_count // STRIDE, STRIDE * feature_count)
    token_stack = doubling(token_piece, 0, sub_bits, device_place, rows_swapper)
    block_rows = token_stack.reshape(row_count, STRIDE * feature_count)
    conv_size = conv_weight.size
    conv_cols = conv_weight.shape[2]
    conv_stack = weight_stack[:, :conv_size].reshape(block_count, STRIDE, feature_count, conv_cols)
    conv_matrix = conv_stack.transpose(1, 2, 0, 3).reshape(
        STRIDE * feature_count, block_count * conv_cols
    )
    head_width = qkv_weight.shape[3]
    proj_matrix = weight_stack[:, conv_size:].reshape(
        block_count * qkv_weight.shape[1], 3 * head_width
    )
    part_sums = jnp.dot(block_rows, conv_matrix, preferred_element_type=jnp.float32)
    coarse_share = lax.psum(part_sums, "head").astype(jnp.bfloat16)
    coarse_stack = doubling(coarse_share, 0, sub_bits, device_place, rows_swapper)
    coarse_full = (
        coarse_stack.reshape(STRIDE, row_count, block_count, conv_cols)
        .transpose(1, 2, 0, 3)
        .reshape(row_count, block_count * conv_cols * STRIDE)
    )
    projected = jnp.dot(coarse_full, proj_matrix, preferred_element_type=jnp.float32).astype(
        jnp.bfloat16
    )
    coarse_q = projected[:, :head_width]
    coarse_pair = jnp.stack(
        [projected[:, head_width : 2 * head_width], projected[:, 2 * head_width :]]
    )
    key_rows, value_rows = window_keys(coarse_pair, COARSE_STEPS, coarse_shifter)
    key_valid = window_valid(row_count, COARSE_STEPS, device_place // STRIDE)
    coarse_mix = attend(coarse_q, key_rows, value_rows, key_valid, HEAD_DIM)
    head_start = (
        device_place % STRIDE * HEADS_SUB + lax.axis_index("head") * (head_width // HEAD_DIM)
    ) * HEAD_DIM
    residual_cols = lax.dynamic_slice_in_dim(coarse_full, head_start, head_width, 1)
    coarse_out = (residual_cols.astype(jnp.float32) + coarse_mix).astype(jnp.bfloat16)
    return (fine_out, coarse_out.reshape(1, row_count, head_width))


def solution(mesh):
    placed = (
        P("ctx", "head"),
        P("ctx", "head"),
        P("ctx", "head"),
        P("ctx", "head"),
        P(None, "head", "ctx"),
        P("ctx", None, None, "head"),
    )
    return jax.shard_map(
        per_device,
        mesh=mesh,
        in_specs=placed,
        out_specs=(P("ctx", "head"), P("ctx", None, "head")),
        check_vma=False,
    )
```

profile of v0, /device:TPU:1, one launch (start us, length us, event | category | flops | bytes accessed | tf_op | source)
XLA Modules:
  0.0 787.0 jit_solution(11338443657087979897)
XLA Ops:
  0.6 1.1 copy.25
  1.9 1.4 copy.24
  4.5 4.5 collective-permute-start.4
  9.0 15.5 %collective-permute-done.4 = bf16[1,229376]{1,0:T(2,128)(2,1)S(1)} collective-permute-done((bf16[1,229376]{1,0:T(2,128)(2,1)S(1)}, bf16[1,229376]{1,0:T(2,128)(2,1)S(1)}, u32[]{:S(2)}, u32[]{:S(2)}) %collective-permute-start.4) | collective-permute-done | bytes 458784 | tf_op jit(solution)/shard_map/ppermute | solution.py:20
  24.5 4.0 broadcast_select_fusion
  28.4 9.4 %collective-permute-start.5 = (bf16[2,229376]{1,0:T(2,128)(2,1)S(1)}, bf16[2,229376]{1,0:T(2,128)(2,1)}, u32[]{:S(2)}, u32[]{:S(2)}) collective-permute-start(bf16[2,229376]{1,0:T(2,128)(2,1)S(1)} %broadcast_select_fusion), channel_id=1, source_target_pairs={{0,64},{64,0},{4,68},{68,4},{8,72},{72,8},{12,76},{76,12},{16,80},... | collective-permute-start | bytes 2752520 | tf_op jit(solution)/shard_map/ppermute | solution.py:20
  37.8 39.5 %collective-permute-done.5 = bf16[2,229376]{1,0:T(2,128)(2,1)} collective-permute-done((bf16[2,229376]{1,0:T(2,128)(2,1)S(1)}, bf16[2,229376]{1,0:T(2,128)(2,1)}, u32[]{:S(2)}, u32[]{:S(2)}) %collective-permute-start.5) | collective-permute-done | bytes 917536 | tf_op jit(solution)/shard_map/ppermute | solution.py:20
  77.4 5.0 maximum_select_fusion.2
  82.4 8.8 %collective-permute-start.6 = (bf16[4,229376]{1,0:T(4,128)(2,1)S(1)}, bf16[4,229376]{1,0:T(4,128)(2,1)}, u32[]{:S(2)}, u32[]{:S(2)}) collective-permute-start(bf16[4,229376]{1,0:T(4,128)(2,1)S(1)} %maximum_select_fusion.2), channel_id=1, source_target_pairs={{0,128},{128,0},{4,132},{132,4},{8,136},{136,8},{12,140},{140,12},... | collective-permute-start | bytes 5505032 | tf_op jit(solution)/shard_map/ppermute | solution.py:20
  91.5 4.8 collective-permute-start
  96.4 231.3 %collective-permute-done.6 = bf16[4,229376]{1,0:T(4,128)(2,1)} collective-permute-done((bf16[4,229376]{1,0:T(4,128)(2,1)S(1)}, bf16[4,229376]{1,0:T(4,128)(2,1)}, u32[]{:S(2)}, u32[]{:S(2)}) %collective-permute-start.6) | collective-permute-done | bytes 1835040 | tf_op jit(solution)/shard_map/ppermute | solution.py:20
  327.7 6.6 maximum_select_fusion.1
  334.3 170.7 %collective-permute-start.7 = (bf16[8,229376]{1,0:T(8,128)(2,1)}, bf16[8,229376]{1,0:T(8,128)(2,1)}, u32[]{:S(2)}, u32[]{:S(2)}) collective-permute-start(bf16[8,229376]{1,0:T(8,128)(2,1)} %maximum_select_fusion.1), channel_id=1, source_target_pairs={{0,256},{256,0},{4,260},{260,4},{8,264},{264,8},{12,268},{268,12},... | collective-permute-start | bytes 11010056 | tf_op jit(solution)/shard_map/ppermute | solution.py:20
  506.8 4.8 collective-permute-start.1
  511.6 2.9 collective-permute-done.1
  514.5 3.1 collective-permute-start.2
  517.6 5.1 collective-permute-done.2
  522.8 4.8 collective-permute-start.3
  527.6 9.7 %collective-permute-done.3 = bf16[4,16,4096]{2,1,0:T(8,128)(2,1)S(1)} collective-permute-done((bf16[4,16,4096]{2,1,0:T(8,128)(2,1)S(1)}, bf16[4,16,4096]{2,1,0:T(8,128)(2,1)S(1)}, u32[]{:S(2)}, u32[]{:S(2)}) %collective-permute-start.3) | collective-permute-done | bytes 524320 | tf_op jit(solution)/shard_map/ppermute | solution.py:20
  537.5 126.0 %collective-permute-done.7 = bf16[8,229376]{1,0:T(8,128)(2,1)} collective-permute-done((bf16[8,229376]{1,0:T(8,128)(2,1)}, bf16[8,229376]{1,0:T(8,128)(2,1)}, u32[]{:S(2)}, u32[]{:S(2)}) %collective-permute-start.7) | collective-permute-done | bytes 3670048 | tf_op jit(solution)/shard_map/ppermute | solution.py:20
  663.5 7.5 maximum_select_fusion
  671.1 2.9 copy-done.2
  674.0 2.3 slice.54
  676.4 22.5 %reshape.204 = bf16[16,8,512,32]{3,2,1,0:T(8,128)(2,1)} reshape(bf16[16,131072]{1,0:T(8,128)(2,1)} %slice.54) | data formatting | bytes 8388608 | tf_op jit(solution)/shard_map/reshape | solution.py:110
  698.9 16.0 %copy.26 = bf16[8,512,16,32]{1,0,3,2:T(8,128)(2,1)} copy(bf16[8,512,16,32]{3,1,0,2:T(8,128)(2,1)} %bitcast.82) | data formatting | bytes 8388608 | tf_op jit(solution)/shard_map/transpose | solution.py:111
  714.9 4.4 copy.35
  719.3 1.5 fusion.72
  720.8 14.9 %all-reduce.1 = bf16[128,512]{1,0:T(8,128)(2,1)S(1)} all-reduce(f32[128,512]{1,0:T(8,128)S(1)} %fusion.72), channel_id=1, replica_groups=mesh['ctx'=128,'head'=4] {'head'}, use_global_device_ids=true, to_apply=%region_2.3 | all-reduce | flops 65536 | bytes 393216 | tf_op jit(solution)/shard_map/psum | solution.py:119
  735.7 4.7 collective-permute-start.8
  740.4 3.3 collective-permute-done.8
  743.7 3.4 collective-permute-start.9
  747.1 5.2 collective-permute-done.9
  752.4 0.9 maximum_select_fusion.6
  753.3 4.8 collective-permute-start.10
  758.9 2.6 reshape.207
  761.5 0.8 copy.29
  762.3 1.2 maximum_select_fusion.10
  763.4 1.8 copy.28
  765.2 1.9 maximum_select_fusion.7
  767.1 1.0 collective-permute-done.10
  768.2 2.0 copy.27
  770.2 1.7 fusion.9
  772.8 1.3 collective-permute-start.11
  774.1 1.3 collective-permute-done.11
  775.4 3.7 collective-permute-start.12
  779.1 1.3 collective-permute-done.12
  780.4 3.7 collective-permute-start.13
  784.1 1.4 collective-permute-done.13
  (61 shorter events, 6.7 us)
Async XLA Ops:
  0.6 505.0 %copy-start = (bf16[128,512]{1,0:T(8,128)(2,1)S(1)}, bf16[128,512]{1,0:T(8,128)(2,1)}, u32[]{:S(2)}) copy-start(bf16[128,512]{1,0:T(8,128)(2,1)} %param.6) | copy-start | bytes 393220
  3.9 87.3 %copy-start.7 = (bf16[128,512]{1,0:T(8,128)(2,1)S(1)}, bf16[128,512]{1,0:T(8,128)(2,1)}, u32[]{:S(2)}) copy-start(bf16[128,512]{1,0:T(8,128)(2,1)} %param.7) | copy-start | bytes 393220
  4.5 86.9 %copy-start.8 = (bf16[128,512]{1,0:T(8,128)(2,1)S(1)}, bf16[128,512]{1,0:T(8,128)(2,1)}, u32[]{:S(2)}) copy-start(bf16[128,512]{1,0:T(8,128)(2,1)} %param.8) | copy-start | bytes 393220
  4.5 20.0 %collective-permute-start.4 = (bf16[1,229376]{1,0:T(2,128)(2,1)S(1)}, bf16[1,229376]{1,0:T(2,128)(2,1)S(1)}, u32[]{:S(2)}, u32[]{:S(2)}) collective-permute-start(bf16[1,229376]{1,0:T(2,128)(2,1)S(1)} %broadcast_in_dim.30), channel_id=1, source_target_pairs={{0,32},{32,0},{4,36},{36,4},{8,40},{40,8},{12,44},{44,12},{16,48},... | collective-permute-start | bytes 1376264 | tf_op jit(solution)/shard_map/ppermute | solution.py:20
  28.4 48.9 %collective-permute-start.5 = (bf16[2,229376]{1,0:T(2,128)(2,1)S(1)}, bf16[2,229376]{1,0:T(2,128)(2,1)}, u32[]{:S(2)}, u32[]{:S(2)}) collective-permute-start(bf16[2,229376]{1,0:T(2,128)(2,1)S(1)} %broadcast_select_fusion), channel_id=1, source_target_pairs={{0,64},{64,0},{4,68},{68,4},{8,72},{72,8},{12,76},{76,12},{16,80},... | collective-permute-start | bytes 2752520 | tf_op jit(solution)/shard_map/ppermute | solution.py:20
  82.4 245.3 %collective-permute-start.6 = (bf16[4,229376]{1,0:T(4,128)(2,1)S(1)}, bf16[4,229376]{1,0:T(4,128)(2,1)}, u32[]{:S(2)}, u32[]{:S(2)}) collective-permute-start(bf16[4,229376]{1,0:T(4,128)(2,1)S(1)} %maximum_select_fusion.2), channel_id=1, source_target_pairs={{0,128},{128,0},{4,132},{132,4},{8,136},{136,8},{12,140},{140,12},... | collective-permute-start | bytes 5505032 | tf_op jit(solution)/shard_map/ppermute | solution.py:20
  91.5 414.0 %collective-permute-start = (bf16[2,128,512]{1,2,0:T(8,128)(2,1)S(1)}, bf16[2,128,512]{1,2,0:T(8,128)(2,1)S(1)}, u32[]{:S(2)}, u32[]{:S(2)}) collective-permute-start(bf16[2,128,512]{1,2,0:T(8,128)(2,1)S(1)} %pad_maximum_fusion.1), channel_id=1, source_target_pairs={{0,4},{4,8},{8,12},{12,16},{16,20},{20,24},{24,28},{28,32},{32,36}... | collective-permute-start | bytes 786440 | tf_op jit(solution)/shard_map/ppermute | solution.py:26
  334.3 172.4 %copy-start.9 = (bf16[128,512]{1,0:T(8,128)(2,1)S(1)}, bf16[128,512]{1,0:T(8,128)(2,1)}, u32[]{:S(2)}) copy-start(bf16[128,512]{1,0:T(8,128)(2,1)} %param.9) | copy-start | bytes 393220
  334.3 329.2 %collective-permute-start.7 = (bf16[8,229376]{1,0:T(8,128)(2,1)}, bf16[8,229376]{1,0:T(8,128)(2,1)}, u32[]{:S(2)}, u32[]{:S(2)}) collective-permute-start(bf16[8,229376]{1,0:T(8,128)(2,1)} %maximum_select_fusion.1), channel_id=1, source_target_pairs={{0,256},{256,0},{4,260},{260,4},{8,264},{264,8},{12,268},{268,12},... | collective-permute-start | bytes 11010056 | tf_op jit(solution)/shard_map/ppermute | solution.py:20
  506.7 20.9 %copy-start.6 = (bf16[128,512]{1,0:T(8,128)(2,1)}, bf16[128,512]{1,0:T(8,128)(2,1)S(1)}, u32[]{:S(2)}) copy-start(bf16[128,512]{1,0:T(8,128)(2,1)S(1)} %add_convert_fusion) | copy-start | bytes 393220
  506.8 7.7 collective-permute-start.1
  514.5 8.2 %collective-permute-start.2 = (bf16[2,16,4096]{2,1,0:T(8,128)(2,1)S(1)}, bf16[2,16,4096]{2,1,0:T(8,128)(2,1)S(1)}, u32[]{:S(2)}, u32[]{:S(2)}) collective-permute-start(bf16[2,16,4096]{2,1,0:T(8,128)(2,1)S(1)} %maximum_select_fusion.8), channel_id=1, source_target_pairs={{0,8},{8,0},{4,12},{12,4},{16,24},{24,16},{20,28},{28,20},{32,40},... | collective-permute-start | bytes 786440 | tf_op jit(solution)/shard_map/ppermute | solution.py:20
  522.8 14.5 %collective-permute-start.3 = (bf16[4,16,4096]{2,1,0:T(8,128)(2,1)S(1)}, bf16[4,16,4096]{2,1,0:T(8,128)(2,1)S(1)}, u32[]{:S(2)}, u32[]{:S(2)}) collective-permute-start(bf16[4,16,4096]{2,1,0:T(8,128)(2,1)S(1)} %maximum_select_fusion.5), channel_id=1, source_target_pairs={{0,16},{16,0},{4,20},{20,4},{8,24},{24,8},{12,28},{28,12},{32,48},... | collective-permute-start | bytes 1572872 | tf_op jit(solution)/shard_map/ppermute | solution.py:20
  671.1 3.0 copy-start.2
  735.7 8.0 %collective-permute-start.8 = (bf16[1,128,512]{2,1,0:T(8,128)(2,1)S(1)}, bf16[1,128,512]{2,1,0:T(8,128)(2,1)S(1)}, u32[]{:S(2)}, u32[]{:S(2)}) collective-permute-start(bf16[1,128,512]{2,1,0:T(8,128)(2,1)S(1)} %bitcast.89), channel_id=1, source_target_pairs={{0,4},{4,0},{8,12},{12,8},{16,20},{20,16},{24,28},{28,24},{32,36},... | collective-permute-start | bytes 393224 | tf_op jit(solution)/shard_map/ppermute | solution.py:20
  743.7 15.2 %slice-start = ((bf16[16,229376]{1,0:T(8,128)(2,1)}), bf16[16,98304]{1,0:T(8,128)(2,1)S(1)}, s32[]{:S(2)}) async-start(bf16[16,229376]{1,0:T(8,128)(2,1)} %copy-done.2), calls=%async_computation | async-start | bytes 6291456 | tf_op jit(solution)/shard_map/slice | solution.py:115
  743.7 8.6 %collective-permute-start.9 = (bf16[2,128,512]{2,1,0:T(8,128)(2,1)S(1)}, bf16[2,128,512]{2,1,0:T(8,128)(2,1)S(1)}, u32[]{:S(2)}, u32[]{:S(2)}) collective-permute-start(bf16[2,128,512]{2,1,0:T(8,128)(2,1)S(1)} %maximum_select_fusion.9), channel_id=1, source_target_pairs={{0,8},{8,0},{4,12},{12,4},{16,24},{24,16},{20,28},{28,20},{32,40},... | collective-permute-start | bytes 786440 | tf_op jit(solution)/shard_map/ppermute | solution.py:20
  752.4 0.9 copy-start.4
  753.3 14.9 %collective-permute-start.10 = (bf16[4,128,512]{2,1,0:T(8,128)(2,1)}, bf16[4,128,512]{2,1,0:T(8,128)(2,1)}, u32[]{:S(2)}, u32[]{:S(2)}) collective-permute-start(bf16[4,128,512]{2,1,0:T(8,128)(2,1)} %maximum_select_fusion.6), channel_id=1, source_target_pairs={{0,16},{16,0},{4,20},{20,4},{8,24},{24,8},{12,28},{28,12},{32,48},... | collective-permute-start | bytes 1572872 | tf_op jit(solution)/shard_map/ppermute | solution.py:20
  758.9 3.4 copy-start.5
  762.3 9.7 %copy-start.3 = (bf16[4096,384]{1,0:T(8,128)(2,1)S(1)}, bf16[4096,384]{1,0:T(8,128)(2,1)}, u32[]{:S(2)}) copy-start(bf16[4096,384]{1,0:T(8,128)(2,1)} %reshape.207) | copy-start | bytes 9437188
  772.0 15.0 %copy-start.1 = (bf16[128,512]{1,0:T(8,128)(2,1)S(1)}, bf16[128,512]{1,0:T(8,128)(2,1)}, u32[]{:S(2)}) copy-start(bf16[128,512]{1,0:T(8,128)(2,1)} %param.6) | copy-start | bytes 393220
  772.8 2.6 collective-permute-start.11
  775.4 5.0 collective-permute-start.12
  780.4 5.1 collective-permute-start.13
where the time goes:
time: 793 us; the launch traced here: 787 us
  waiting for transfers between devices  444 us (56%)
  starting transfers between devices  232 us (29%)
  local copies, waits for them, and re-layouts  61.5 us (8%)
  other arithmetic  29.7 us (4%)
  blocking collectives  14.9 us (2%)
    ppermute x10, waiting for transfers between devices, partner_2(): return lax.ppermute(block, axis, route)  440 us
    ppermute x10, starting transfers between devices, partner_2(): return lax.ppermute(block, axis, route)  219 us
    select_n x11, other arithmetic, doubling(): jnp.where(upper_half, jnp.concatenate([partner, gathered], 0), jnp.concat...  27.4 us
    reshape x1, local copies, waits for them, and re-layouts, per_device(): weight_stack[:, :conv_size]  22.5 us
    transpose x1, local copies, waits for them, and re-layouts, per_device(): conv_stack.transpose(1, 2, 0, 3)  16 us
  transfers between devices with their start and end apart: 14, of which 13 were waited for; matrix products, arithmetic and copies ran while one was open for 2% of the time, Pallas kernels for 0%

commit v1 on v0

v1 whole, which is shorter than its diff:
```python
import jax
import jax.numpy as jnp
from jax import lax
from jax.experimental import pallas as pl
from jax.experimental.pallas import tpu as pltpu
from jax.sharding import PartitionSpec as P

STRIDE = 8
HEAD_DIM = 128
NZ = 16
MESH = pl.DeviceIdType.MESH
BF16 = jnp.bfloat16
F32 = jnp.float32
SCALE = HEAD_DIM ** -0.5
NEG = -1e30
GROUPS = ((0, 1), (2, 3), (4, 5), (6,), (7,))
TO_RIGHT = (7, 8, 8)
SHIFT = (0, 1, 1)
ORDER = (1, 2, 0)


def slot_of(offset):
    if offset == -8:
        offset = 8
    return -offset if offset <= 0 else 7 + offset


def dot_t(a, b):
    return lax.dot_general(a, b, (((1,), (1,)), ((), ())), preferred_element_type=F32)


def dot(a, b):
    return jnp.dot(a, b, preferred_element_type=F32)


def whole_wait(ref, sem):
    pltpu.make_async_copy(ref, ref, sem).wait()


def kernel(
    q_in, k_in, v_in, x_in, cw_in, pw_in, fine_out, coarse_out,
    q_v, k_v, v_v, x_v, pk_v, pv_v, mix_v, fo_v, ts_v, acts, wt_v, w2_v, pw_v, p2_v,
    sb_v, rb_v, gs_v, gb_v, cc_v, pr_v, rr_v, rl_v, sr_v, sl_v, r1_v, res_v, xs_v, f_v, kv_v, co_v,
    in_sem, fs, fr, ws, wr, as_, ar, zs, zr, ss, sr, gs, gr, rs_s, rs_r, r1s, r1r, xs, xr, ks, kr, out_sem,
):
    ctx = lax.axis_index("ctx")
    head = lax.axis_index("head")
    z = lax.div(ctx, 8)
    s = lax.rem(ctx, 8)
    yl = lax.div(head, 2)
    core = lax.rem(head, 2)
    chip = 2 * s + yl
    half = lax.div(s, 4)
    quarter = lax.rem(s, 4)
    sibling = (ctx, 2 * yl + 1 - core)
    after = (lax.rem(ctx + 1, 128), head)
    before = (lax.rem(ctx + 127, 128), head)
    right = (lax.rem(z + 1, NZ) * 8 + s, head)
    left = (lax.rem(z + NZ - 1, NZ) * 8 + s, head)
    zt = lax.rem(chip - z + NZ, NZ)
    far = (zt * 8 + s, head)

    chips = []
    for j in range(1, 16):
        c = lax.rem(chip + j, 16)
        chips.append((c, (z * 8 + lax.div(c, 2), lax.rem(c, 2) * 2 + core)))
    subs = [lax.rem(s + j, 8) for j in range(1, 8)]
    res_chip = (z * 8 + lax.div(zt, 2), lax.rem(zt, 2) * 2 + core)

    def remote(src, dst, send, recv, dev):
        cp = pltpu.make_async_remote_copy(
            src_ref=src, dst_ref=dst, send_sem=send, recv_sem=recv, device_id=dev, device_id_type=MESH
        )
        cp.start()
        return cp

    loads = []
    for i, (src, dst) in enumerate([(q_in, q_v), (k_in, k_v), (v_in, v_v), (x_in, x_v)]):
        cp = pltpu.make_async_copy(src, dst, in_sem.at[i])
        cp.start()
        loads.append(cp)

    barrier = pltpu.get_barrier_semaphore()

    def greet(dev):
        pl.semaphore_signal(barrier, inc=1, device_id=dev, device_id_type=MESH)

    for dev in (after, before, right, left, sibling):
        greet(dev)

    for _, dev in chips:
        greet(dev)
    for to in subs:
        greet((z * 8 + to, 2 * yl + 1 - core))

    @pl.when(zt != z)
    def _():
        greet(far)

    pl.semaphore_wait(barrier, 27 + jnp.where(zt != z, 1, 0))

    k_cp = remote(k_in, pk_v, fs.at[0], fr.at[0], after)
    v_cp = remote(v_in, pv_v, fs.at[1], fr.at[1], after)

    row = lax.broadcasted_iota(jnp.int32, (128, 128), 0)
    col = lax.broadcasted_iota(jnp.int32, (128, 128), 1)
    causal = col <= row
    for cp in loads:
        cp.wait()
    k_cp.wait_recv()
    v_cp.wait_recv()

    for to in subs:
        remote(cw_in.at[to], wt_v.at[core, s], ws.at[0], wr.at[0], (z * 8 + to, head))
    pltpu.make_async_copy(cw_in.at[s], wt_v.at[core, s], wr.at[0]).start()
    pw_cp = remote(pw_in, pw_v.at[core], ws.at[1], wr.at[1], sibling)
    pw_own = pltpu.make_async_copy(pw_in, pw_v.at[core], wr.at[2])
    pw_own.start()

    has_before = ctx > 0
    for i in range(4):
        cols = slice(i * 128, (i + 1) * 128)
        q = q_v[:, cols]
        own = jnp.where(causal, dot_t(q, k_v[:, cols]) * SCALE, NEG)
        prev = jnp.where(has_before, dot_t(q, pk_v[:, cols]) * SCALE, NEG)
        top = jnp.maximum(jnp.max(own, 1, keepdims=True), jnp.max(prev, 1, keepdims=True))
        e_own = jnp.exp(own - top)
        e_prev = jnp.exp(prev - top)
        total = jnp.sum(e_own, 1, keepdims=True) + jnp.sum(e_prev, 1, keepdims=True)
        mixed = dot(e_own.astype(BF16), v_v[:, cols]) + dot(e_prev.astype(BF16), pv_v[:, cols])
        mix_v[i] = x_v[:, cols].astype(F32) + mixed / total
    for tap in range(8):
        for i in range(4):
            ts_v[tap, :, i * 128 : (i + 1) * 128] = mix_v[i, pl.ds(tap, 16, stride=8), :].astype(BF16)

    for to in subs:
        remote(ts_v.at[to], acts.at[0, core, quarter], as_.at[0], ar.at[0], (z * 8 + to, 2 * yl + half))

    @pl.when(core == half)
    def _():
        pltpu.make_async_copy(ts_v.at[s], acts.at[0, core, quarter], ar.at[0]).start()

    @pl.when(core != half)
    def _():
        remote(ts_v.at[s], acts.at[0, core, quarter], as_.at[1], ar.at[0], sibling)

    for i in range(4):
        fo_v[:, i * 128 : (i + 1) * 128] = mix_v[i].astype(BF16)
    fo_cp = pltpu.make_async_copy(fo_v, fine_out, out_sem.at[0])
    fo_cp.start()

    whole_wait(acts.at[0], ar.at[0])
    to_right = {}
    to_left = {}

    def pass_right(k, part):
        a, b = slot_of(-(k - 1)), slot_of(-k)
        to_right[k, part] = remote(
            acts.at[a, part], acts.at[b, part], zs.at[0, k - 1, part], zr.at[0, k - 1, part], right
        )

    def pass_left(k, part):
        a, b = slot_of(k - 1), slot_of(k)
        to_left[k, part] = remote(
            acts.at[a, part], acts.at[b, part], zs.at[1, k - 1, part], zr.at[1, k - 1, part], left
        )

    for part in range(2):
        pass_right(1, part)
        pass_left(1, part)

    whole_wait(wt_v.at[core], wr.at[0])
    wt_cp = remote(wt_v.at[core], wt_v.at[core], ws.at[2], wr.at[3], sibling)
    pw_own.wait()
    whole_wait(pw_v.at[1 - core], wr.at[1])
    for m in range(3):
        for part in range(2):
            at = m * 256 + part * 128
            p2_v[:, at : at + 128] = pw_v[part, m]
    whole_wait(wt_v.at[1 - core], wr.at[3])
    for part in range(2):
        w2_v[part] = wt_v[part].reshape(256, 512).T

    def group_slots(pairs):
        return [slot_of(o) for p in pairs for o in (-p, p + 1)]

    def conv(g):
        pairs = GROUPS[g]
        n, at = len(pairs), pairs[0]
        total = None
        for part in range(2):
            rows = jnp.concatenate([acts[a, part].reshape(64, 512) for a in group_slots(pairs)], 0)
            term = dot(rows, w2_v[part])
            total = term if total is None else total + term
        for i in range(n):
            lo = total[i * 128 : (i + 1) * 128, :128].reshape(16, 8, 128)
            hi = total[i * 128 : (i + 1) * 128, 128:].reshape(16, 8, 128)
            sb_v[:, at + i] = jnp.concatenate([lo, hi], 1).astype(BF16)
        span = pl.ds(at, n)
        for to, dev in chips:
            remote(sb_v.at[to, span], rb_v.at[chip, span], ss.at[g], sr.at[g], dev)
        pltpu.make_async_copy(sb_v.at[chip, span], rb_v.at[chip, span], sr.at[g]).start()

    def reduce(g):
        n, at = len(GROUPS[g]), GROUPS[g][0]
        span = pl.ds(at, n)
        whole_wait(rb_v.at[:, span], sr.at[g])
        gs_v[at : at + n] = jnp.sum(rb_v[:, at : at + n].astype(F32), 0).astype(BF16)
        for _, dev in chips:
            remote(gs_v.at[span], gb_v.at[chip, span], gs.at[g], gr.at[g], dev)
        pltpu.make_async_copy(gs_v.at[span], gb_v.at[chip, span], gr.at[g]).start()

    def project(g):
        pairs = GROUPS[g]
        n, at = len(pairs), pairs[0]
        whole_wait(gb_v.at[:, pl.ds(at, n)], gr.at[g])
        blocks = []
        for i in range(n):
            got = gb_v[:, at + i].astype(F32)
            blocks.append(jnp.concatenate([got[:, :8].reshape(128, 128), got[:, 8:].reshape(128, 128)], 1))
        rows = jnp.concatenate(blocks, 0).astype(BF16)
        terms = dot(rows, p2_v[...])
        for i, a in enumerate(group_slots(pairs)):
            cc_v[a] = rows[i * 64 : (i + 1) * 64]
            for m in range(3):
                pr_v[a, m] = terms[i * 64 : (i + 1) * 64, m * 256 : (m + 1) * 256]

    def ring(step):
        for part in range(2):
            if step <= 7 or part == 0:
                to_right[step, part].wait_recv()
                if step < 7 or (step == 7 and part == 0):
                    pass_right(step + 1, part)
            if step <= 7 or part == 1:
                to_left[step, part].wait_recv()
                if step < 7 or (step == 7 and part == 1):
                    pass_left(step + 1, part)

    ring(1)
    ring(2)
    conv(0)
    ring(3)
    ring(4)
    conv(1)
    reduce(0)
    ring(5)
    project(0)
    ring(6)
    conv(2)
    reduce(1)
    ring(7)
    conv(3)
    reduce(2)
    project(1)
    ring(8)
    conv(4)
    reduce(3)
    project(2)
    reduce(4)
    project(3)

    sums_right = {}
    sums_left = {}

    def add_right(k, m):
        term = pr_v[slot_of(TO_RIGHT[m] - SHIFT[m] - k), m]
        if k:
            sums_right[k, m].wait_recv()
            term = rr_v[k - 1, m].astype(F32) + term
        sr_v[k, m] = term.astype(BF16)
        sums_right[k + 1, m] = remote(sr_v.at[k, m], rr_v.at[k, m], rs_s.at[0, k, m], rs_r.at[0, k, m], right)

    def add_left(k, m):
        term = pr_v[slot_of(k - (15 - TO_RIGHT[m]) - SHIFT[m]), m]
        if k:
            sums_left[k, m].wait_recv()
            term = rl_v[k - 1, m].astype(F32) + term
        sl_v[k, m] = term.astype(BF16)
        sums_left[k + 1, m] = remote(sl_v.at[k, m], rl_v.at[k, m], rs_s.at[1, k, m], rs_r.at[1, k, m], left)

    for m in ORDER:
        add_right(0, m)
    project(4)
    for m in ORDER:
        add_left(0, m)

    offset = lax.rem(zt - z + NZ, NZ)
    place = jnp.where(offset == 0, 0, jnp.where(offset <= 8, 7 + offset, NZ - offset))

    @pl.when(zt != z)
    def _():
        remote(cc_v.at[place], r1_v, r1s.at[0], r1r.at[0], far)

    @pl.when(zt == z)
    def _():
        pltpu.make_async_copy(cc_v.at[place], r1_v, r1r.at[0]).start()

    k_cp.wait_send()
    v_cp.wait_send()
    whole_wait(wt_v.at[0, pl.ds(0, 7)], ws.at[0])
    pw_cp.wait_send()
    wt_cp.wait_send()
    whole_wait(ts_v.at[pl.ds(0, 7)], as_.at[0])

    @pl.when(core != half)
    def _():
        whole_wait(ts_v.at[0], as_.at[1])

    for cp in list(to_right.values()) + list(to_left.values()):
        cp.wait_send()
    for g, pairs in enumerate(GROUPS):
        whole_wait(sb_v.at[pl.ds(0, 15), pl.ds(pairs[0], len(pairs))], ss.at[g])

    for k in range(1, 8):
        for m in ORDER:
            if k < TO_RIGHT[m]:
                add_right(k, m)
            if k < 15 - TO_RIGHT[m]:
                add_left(k, m)
        if k == 4:
            whole_wait(r1_v, r1r.at[0])

            @pl.when(z != 0)
            def _():
                remote(r1_v, res_v, r1s.at[1], r1r.at[1], res_chip)

            @pl.when(z == 0)
            def _():
                pltpu.make_async_copy(r1_v, res_v, r1r.at[1]).start()
            for g, pairs in enumerate(GROUPS):
                whole_wait(sb_v.at[pl.ds(0, 15), pl.ds(pairs[0], len(pairs))], gs.at[g])

    first = core == 0

    def exchange(m, both):
        f_v[m, core] = jnp.where(first, both[:, :128], both[:, 128:])
        xs_v[m] = jnp.where(first, both[:, 128:], both[:, :128])
        return remote(xs_v.at[m], f_v.at[m, core], xs.at[m], xr.at[m], sibling)

    whole_wait(res_v, r1r.at[1])
    swaps = {3: exchange(3, res_v[...])}
    for m in ORDER:
        nr = TO_RIGHT[m]
        sums_right[nr, m].wait_recv()
        sums_left[15 - nr, m].wait_recv()
        both = pr_v[slot_of(-SHIFT[m]), m] + rr_v[nr - 1, m].astype(F32) + rl_v[14 - nr, m].astype(F32)
        swaps[m] = exchange(m, both.astype(BF16))
    kv_cp = {}
    for i in range(2):
        whole_wait(f_v.at[1 + i, 1 - core], xr.at[1 + i])
        kv_cp[1, i] = remote(f_v.at[1 + i], kv_v.at[1, i], ks.at[1, i], kr.at[1, i], right)
        kv_cp[0, i] = remote(f_v.at[1 + i], kv_v.at[0, i], ks.at[0, i], kr.at[0, i], left)
    for cp in list(sums_right.values()) + list(sums_left.values()):
        cp.wait_send()

    @pl.when(zt != z)
    def _():
        whole_wait(r1_v, r1s.at[0])

    @pl.when(z != 0)
    def _():
        whole_wait(r1_v, r1s.at[1])

    whole_wait(f_v.at[0, 1 - core], xr.at[0])
    whole_wait(f_v.at[3, 1 - core], xr.at[3])
    for cp in swaps.values():
        cp.wait_send()
    for i in range(2):
        kv_cp[1, i].wait_recv()
        kv_cp[2, i] = remote(kv_v.at[1, i], kv_v.at[2, i], ks.at[2, i], kr.at[2, i], right)
    for i in range(2):
        kv_cp[0, i].wait_recv()
    for i in range(2):
        kv_cp[2, i].wait_recv()

    q = f_v[0].reshape(128, 128)
    keys, vals = [
        [ref[...].reshape(128, 128) for ref in (kv_v.at[0, i], f_v.at[1 + i], kv_v.at[1, i], kv_v.at[2, i])]
        for i in range(2)
    ]
    scores = []
    for back in range(4):
        seen = causal if back == 0 else z >= back
        scores.append(jnp.where(seen, dot_t(q, keys[back]) * SCALE, NEG))
    top = scores[0].max(1, keepdims=True)
    for back in range(1, 4):
        top = jnp.maximum(top, scores[back].max(1, keepdims=True))
    total = None
    mixed = None
    for back in range(4):
        e = jnp.exp(scores[back] - top)
        part_sum = jnp.sum(e, 1, keepdims=True)
        part_mix = dot(e.astype(BF16), vals[back])
        total = part_sum if total is None else total + part_sum
        mixed = part_mix if mixed is None else mixed + part_mix
    co_v[...] = (f_v[3].reshape(128, 128).astype(F32) + mixed / total).astype(BF16)
    co_cp = pltpu.make_async_copy(co_v, coarse_out.at[0], out_sem.at[1])
    co_cp.start()

    for cp in kv_cp.values():
        cp.wait_send()
    fo_cp.wait()
    co_cp.wait()


def per_device(fine_q, fine_k, fine_v, fine_x, conv_weight, qkv_weight):
    cw = conv_weight.transpose(0, 2, 1)
    pw = qkv_weight[0].transpose(1, 0, 2)
    dma = pltpu.SemaphoreType.DMA
    vmem = pltpu.VMEM
    scratch = [
        vmem((128, 512), BF16), vmem((128, 512), BF16), vmem((128, 512), BF16), vmem((128, 512), BF16),
        vmem((128, 512), BF16), vmem((128, 512), BF16),
        vmem((4, 128, 128), F32),
        vmem((128, 512), BF16),
        vmem((8, 16, 512), BF16),
        vmem((16, 2, 4, 16, 512), BF16),
        vmem((2, 8, 32, 512), BF16),
        vmem((2, 512, 256), BF16),
        vmem((2, 3, 256, 128), BF16),
        vmem((256, 768), BF16),
        vmem((16, 8, 16, 128), BF16),
        vmem((16, 8, 16, 128), BF16),
        vmem((8, 16, 128), BF16),
        vmem((16, 8, 16, 128), BF16),
        vmem((16, 64, 256), BF16),
        vmem((16, 3, 64, 256), F32),
        vmem((8, 3, 64, 256), BF16),
        vmem((8, 3, 64, 256), BF16),
        vmem((8, 3, 64, 256), BF16),
        vmem((8, 3, 64, 256), BF16),
        vmem((64, 256), BF16),
        vmem((64, 256), BF16),
        vmem((4, 64, 128), BF16),
        vmem((4, 2, 64, 128), BF16),
        vmem((3, 2, 2, 64, 128), BF16),
        vmem((128, 128), BF16),
        dma((4,)), dma((2,)), dma((2,)), dma((3,)), dma((4,)), dma((2,)), dma((1,)),
        dma((2, 8, 2)), dma((2, 8, 2)),
        dma((5,)), dma((5,)), dma((5,)), dma((5,)),
        dma((2, 8, 3)), dma((2, 8, 3)),
        dma((2,)), dma((2,)), dma((4,)), dma((4,)),
        dma((3, 2)), dma((3, 2)), dma((2,)),
    ]
    return pl.pallas_call(
        kernel,
        out_shape=(
            jax.ShapeDtypeStruct((128, 512), BF16),
            jax.ShapeDtypeStruct((1, 128, 128), BF16),
        ),
        in_specs=[pl.BlockSpec(memory_space=pl.ANY)] * 6,
        out_specs=[pl.BlockSpec(memory_space=pl.ANY)] * 2,
        scratch_shapes=scratch,
        compiler_params=pltpu.CompilerParams(
            collective_id=0, has_side_effects=True, vmem_limit_bytes=60 * 1024 * 1024
        ),
    )(fine_q, fine_k, fine_v, fine_x, cw, pw)


def solution(mesh):
    placed = (
        P("ctx", "head"),
        P("ctx", "head"),
        P("ctx", "head"),
        P("ctx", "head"),
        P(None, "head", "ctx"),
        P("ctx", None, None, "head"),
    )
    return jax.shard_map(
        per_device,
        mesh=mesh,
        in_specs=placed,
        out_specs=(P("ctx", "head"), P("ctx", None, "head")),
        check_vma=False,
    )
```

time: 793 us -> 117 us (0.15)
  waiting for transfers between devices: 444 us -> 0 us
  starting transfers between devices: 232 us -> 0 us
  Pallas kernels: 0 us -> 113 us
  local copies, waits for them, and re-layouts: 61.5 us -> 2.19 us
  other arithmetic: 29.7 us -> 0 us
  blocking collectives: 14.9 us -> 0 us
    ppermute x14 -> x0, waiting for transfers between devices: 444 us -> none  [the longest x10 440 us: partner_2(): return lax.ppermute(block, axis, route)]
    ppermute x14 -> x0, starting transfers between devices: 232 us -> none  [the longest x10 219 us: partner_2(): return lax.ppermute(block, axis, route)]
    pallas_call x0 -> x1, Pallas kernels: none -> 113 us  [per_device(): pl.pallas_call(kernel, out_shape=(jax.ShapeDtypeStruct((128, 512), BF16),...]
    select_n x11 -> x0, other arithmetic: 27.4 us -> none  [doubling(): jnp.where(upper_half, jnp.concatenate([partner, gathered], 0), jnp.concat...]
    reshape x5 -> x0, local copies, waits for them, and re-layouts: 25.9 us -> none  [the longest x1 22.5 us: per_device(): weight_stack[:, :conv_size]]
    transpose x2 -> x0, local copies, waits for them, and re-layouts: 16.1 us -> none  [the longest x1 16 us: per_device(): conv_stack.transpose(1, 2, 0, 3)]
    psum x1 -> x0, blocking collectives: 14.9 us -> none  [per_device(): coarse_share = lax.psum(part_sums, 'head').astype(jnp.bfloat16)]
    unnamed x26 -> x4, local copies, waits for them, and re-layouts: 10.9 us -> 2.19 us
  transfers between devices with their start and end apart: 14 -> 0, of which waited for: 13 -> 0; matrix products, arithmetic and copies ran while one was open for 2% -> 0% of each run, Pallas kernels for 0% -> 0%
where the time goes in v1:
time: 117 us; the launch traced here: 116 us
  Pallas kernels  113 us (97%)
  local copies, waits for them, and re-layouts  2.19 us (2%)
    pallas_call x1, Pallas kernels, per_device(): pl.pallas_call(kernel, out_shape=(jax.ShapeDtypeStruct((128, 512), BF16),...  113 us

profile of v1, /device:TPU:1, one launch (start us, length us, event | category | flops | bytes accessed | tf_op | source)
XLA Modules:
  0.0 115.8 jit_solution(3592956879384146076)
XLA Ops:
  0.6 112.9 %shard_map.77 = (bf16[128,512]{1,0:T(8,128)(2,1)}, bf16[1,128,128]{2,1,0:T(8,128)(2,1)}) custom-call(bf16[128,512]{1,0:T(8,128)(2,1)} %q_in.1, bf16[128,512]{1,0:T(8,128)(2,1)} %k_in.1, bf16[128,512]{1,0:T(8,128)(2,1)} %v_in.1, bf16[128,512]{1,0:T(8,128)(2,1)} %x_in.1, bf16[8,32,512]{2,1,0:T(8,128)(2,1)} %bitcast.4, bf16[3,256,128]{2,1,0:T(8,128)(2,1)} %bitcast.5), custom_call_target="tpu_custom_call" | custom-call | tf_op jit(solution)/shard_map/pallas_call | solution.py:445
  113.6 0.0 copy-start
  113.6 1.6 %copy.10 = bf16[128,512]{1,0:T(8,128)(2,1)} copy(bf16[128,512]{1,0:T(8,128)(2,1)} %get-tuple-element.4) | data formatting | bytes 262144
  115.2 0.0 copy-done
  115.2 0.6 copy.11
Async XLA Ops:
  113.6 1.6 %copy-start = (bf16[1,128,128]{2,1,0:T(8,128)(2,1)S(1)}, bf16[1,128,128]{2,1,0:T(8,128)(2,1)}, u32[]{:S(2)}) copy-start(bf16[1,128,128]{2,1,0:T(8,128)(2,1)} %get-tuple-element.5) | copy-start | bytes 98308

commit v2 on v1

v2 whole, which is shorter than its diff:
```python
import jax
import jax.numpy as jnp
from jax import lax
from jax.experimental import pallas as pl
from jax.experimental.pallas import tpu as pltpu
from jax.sharding import PartitionSpec as P

STRIDE = 8
HEAD_DIM = 128
NZ = 16
MESH = pl.DeviceIdType.MESH
BF16 = jnp.bfloat16
F32 = jnp.float32
SCALE = HEAD_DIM ** -0.5
NEG = -1e30
GROUPS = ((0, 1), (2, 3), (4, 5), (6,), (7,))
TO_RIGHT = (7, 8, 8)
SHIFT = (0, 1, 1)
ORDER = (1, 2, 0)


def slot_of(offset):
    if offset == -8:
        offset = 8
    return -offset if offset <= 0 else 7 + offset


def dot_t(a, b):
    return lax.dot_general(a, b, (((1,), (1,)), ((), ())), preferred_element_type=F32)


def dot(a, b):
    return jnp.dot(a, b, preferred_element_type=F32)


def whole_wait(ref, sem):
    pltpu.make_async_copy(ref, ref, sem).wait()


def kernel(
    q_in, k_in, v_in, x_in, cw_in, pw_in, fine_out, coarse_out,
    q_v, k_v, v_v, x_v, pk_v, pv_v, mix_v, fo_v, ts_v, acts, wt_v, w2_v, pw_v, p2_v,
    sb_v, rb_v, gs_v, gb_v, cc_v, pr_v, rr_v, rl_v, sr_v, sl_v, r1_v, res_v, xs_v, f_v, ys_v, kv_v, co_v,
    in_sem, fs, fr, ws, wr, as_, ar, zs, zr, ss, sr, gs, gr, rs_s, rs_r, r1s, r1r, xs, xr, ks, kr, out_sem,
):
    ctx = lax.axis_index("ctx")
    head = lax.axis_index("head")
    z = lax.div(ctx, 8)
    s = lax.rem(ctx, 8)
    yl = lax.div(head, 2)
    core = lax.rem(head, 2)
    chip = 2 * s + yl
    half = lax.div(s, 4)
    quarter = lax.rem(s, 4)
    sibling = (ctx, 2 * yl + 1 - core)
    after = (lax.rem(ctx + 1, 128), head)
    before = (lax.rem(ctx + 127, 128), head)
    right = (lax.rem(z + 1, NZ) * 8 + s, head)
    left = (lax.rem(z + NZ - 1, NZ) * 8 + s, head)
    zt = lax.rem(chip - z + NZ, NZ)
    far = (zt * 8 + s, head)

    chips = []
    for j in range(1, 16):
        c = lax.rem(chip + j, 16)
        chips.append((c, (z * 8 + lax.div(c, 2), lax.rem(c, 2) * 2 + core)))
    subs = [lax.rem(s + j, 8) for j in range(1, 8)]
    res_chip = (z * 8 + lax.div(zt, 2), lax.rem(zt, 2) * 2 + core)

    def plane_at(away, c):
        return (lax.rem(z + away, NZ) * 8 + s, 2 * yl + c)

    def remote(src, dst, send, recv, dev):
        cp = pltpu.make_async_remote_copy(
            src_ref=src, dst_ref=dst, send_sem=send, recv_sem=recv, device_id=dev, device_id_type=MESH
        )
        cp.start()
        return cp

    loads = []
    for i, (src, dst) in enumerate([(q_in, q_v), (k_in, k_v), (v_in, v_v), (x_in, x_v)]):
        cp = pltpu.make_async_copy(src, dst, in_sem.at[i])
        cp.start()
        loads.append(cp)

    barrier = pltpu.get_barrier_semaphore()

    def greet(dev):
        pl.semaphore_signal(barrier, inc=1, device_id=dev, device_id_type=MESH)

    for dev in (after, before):
        greet(dev)
    for away in (1, 2, NZ - 2, NZ - 1):
        for c in range(2):
            greet(plane_at(away, c))

    for _, dev in chips:
        greet(dev)
    greet(sibling)
    for to in subs:
        greet((z * 8 + to, 2 * yl + 1 - core))

    @pl.when(zt != z)
    def _():
        greet(far)

    pl.semaphore_wait(barrier, 33 + jnp.where(zt != z, 1, 0))

    fine_cp = []
    for hp in range(2):
        cols = pl.ds(hp * 256, 256)
        for i, (src, dst) in enumerate([(k_in, pk_v), (v_in, pv_v)]):
            fine_cp.append(remote(src.at[:, cols], dst.at[hp], fs.at[2 * hp + i], fr.at[2 * hp + i], after))

    row = lax.broadcasted_iota(jnp.int32, (128, 128), 0)
    col = lax.broadcasted_iota(jnp.int32, (128, 128), 1)
    causal = col <= row
    for cp in loads:
        cp.wait()
    own_part = []
    for i in range(4):
        cols = slice(i * 128, (i + 1) * 128)
        scores = jnp.where(causal, dot_t(q_v[:, cols], k_v[:, cols]) * SCALE, NEG)
        top = jnp.max(scores, 1, keepdims=True)
        e = jnp.exp(scores - top)
        mix_v[i] = dot(e.astype(BF16), v_v[:, cols])
        own_part.append((top, jnp.sum(e, 1, keepdims=True)))
    has_before = ctx > 0
    for hp in range(2):
        fine_cp[2 * hp].wait_recv()
        fine_cp[2 * hp + 1].wait_recv()
        for j in range(2):
            i = 2 * hp + j
            cols = slice(i * 128, (i + 1) * 128)
            near = slice(j * 128, (j + 1) * 128)
            scores = jnp.where(has_before, dot_t(q_v[:, cols], pk_v[hp, :, near]) * SCALE, NEG)
            own_top, own_sum = own_part[i]
            top = jnp.maximum(own_top, jnp.max(scores, 1, keepdims=True))
            scale = jnp.exp(own_top - top)
            e = jnp.exp(scores - top)
            total = own_sum * scale + jnp.sum(e, 1, keepdims=True)
            mixed = mix_v[i] * scale + dot(e.astype(BF16), pv_v[hp, :, near])
            mix_v[i] = x_v[:, cols].astype(F32) + mixed / total
            for tap in range(8):
                ts_v[hp, tap, :, near] = mix_v[i, pl.ds(tap, 16, stride=8), :].astype(BF16)
        for to in subs:
            remote(
                ts_v.at[hp, to], acts.at[0, hp, core, quarter], as_.at[hp], ar.at[hp], (z * 8 + to, 2 * yl + half)
            )

        @pl.when(core == half)
        def _():
            pltpu.make_async_copy(ts_v.at[hp, s], acts.at[0, hp, core, quarter], ar.at[hp]).start()

        @pl.when(core != half)
        def _():
            remote(ts_v.at[hp, s], acts.at[0, hp, core, quarter], as_.at[2 + hp], ar.at[hp], sibling)

    to_right = {}
    to_left = {}
    parts = [(hp, c) for hp in range(2) for c in range(2)]

    def pass_right(k, hp, c):
        a, b = slot_of(-(k - 1)), slot_of(-k)
        to_right[k, hp, c] = remote(
            acts.at[a, hp, c], acts.at[b, hp, c], zs.at[0, k - 1, hp, c], zr.at[0, k - 1, hp, c], right
        )

    def pass_left(k, hp, c):
        a, b = slot_of(k - 1), slot_of(k)
        to_left[k, hp, c] = remote(
            acts.at[a, hp, c], acts.at[b, hp, c], zs.at[1, k - 1, hp, c], zr.at[1, k - 1, hp, c], left
        )

    for hp in range(2):
        whole_wait(acts.at[0, hp], ar.at[hp])
        for c in range(2):
            pass_right(1, hp, c)
            pass_left(1, hp, c)

    for to in subs:
        remote(cw_in.at[to], wt_v.at[core, s], ws.at[0], wr.at[0], (z * 8 + to, head))
    pltpu.make_async_copy(cw_in.at[s], wt_v.at[core, s], wr.at[0]).start()
    pw_cp = remote(pw_in, pw_v.at[core], ws.at[1], wr.at[1], sibling)
    pw_own = pltpu.make_async_copy(pw_in, pw_v.at[core], wr.at[2])
    pw_own.start()
    for i in range(4):
        fo_v[:, i * 128 : (i + 1) * 128] = mix_v[i].astype(BF16)
    fo_cp = pltpu.make_async_copy(fo_v, fine_out, out_sem.at[0])
    fo_cp.start()

    pieces = []
    kept = {}

    def piece(ready):
        def add(f):
            pieces.append((ready, f))
            return f

        return add

    @piece(3)
    def _():
        whole_wait(wt_v.at[core], wr.at[0])
        kept["wt"] = remote(wt_v.at[core], wt_v.at[core], ws.at[2], wr.at[3], sibling)

    @piece(3)
    def _():
        pw_own.wait()
        whole_wait(pw_v.at[1 - core], wr.at[1])
        for m in range(3):
            for part in range(2):
                at = m * 256 + part * 128
                p2_v[:, at : at + 128] = pw_v[part, m]

    def turn(c, hp):
        w2_v[c, hp * 256 : (hp + 1) * 256, :] = wt_v[c, :, :, hp * 256 : (hp + 1) * 256].reshape(256, 256).T

    @piece(4)
    def _():
        turn(core, 0)

    @piece(5)
    def _():
        turn(core, 1)

    @piece(6)
    def _():
        whole_wait(wt_v.at[1 - core], wr.at[3])
        turn(1 - core, 0)

    @piece(7)
    def _():
        turn(1 - core, 1)

    def group_slots(pairs):
        return [slot_of(o) for p in pairs for o in (-p, p + 1)]

    def in_thirds(ready, send):
        for third in range(3):

            @piece(ready)
            def _(third=third):
                for to, dev in chips[5 * third : 5 * third + 5]:
                    send(to, dev)

    def conv(g, ready):
        pairs = GROUPS[g]
        n, at = len(pairs), pairs[0]
        span = pl.ds(at, n)

        @piece(ready)
        def _():
            total = None
            for hp, c in parts:
                rows = jnp.concatenate([acts[a, hp, c].reshape(64, 256) for a in group_slots(pairs)], 0)
                term = dot(rows, w2_v[c, hp * 256 : (hp + 1) * 256, :])
                total = term if total is None else total + term
            for i in range(n):
                lo = total[i * 128 : (i + 1) * 128, :128].reshape(16, 8, 128)
                hi = total[i * 128 : (i + 1) * 128, 128:].reshape(16, 8, 128)
                sb_v[:, at + i] = jnp.concatenate([lo, hi], 1).astype(BF16)
            pltpu.make_async_copy(sb_v.at[chip, span], rb_v.at[chip, span], sr.at[g]).start()

        in_thirds(
            ready, lambda to, dev: remote(sb_v.at[to, span], rb_v.at[chip, span], ss.at[g], sr.at[g], dev)
        )

    def reduce(g, ready):
        n, at = len(GROUPS[g]), GROUPS[g][0]
        span = pl.ds(at, n)

        @piece(ready)
        def _():
            whole_wait(rb_v.at[:, span], sr.at[g])
            gs_v[at : at + n] = jnp.sum(rb_v[:, at : at + n].astype(F32), 0).astype(BF16)
            pltpu.make_async_copy(gs_v.at[span], gb_v.at[chip, span], gr.at[g]).start()

        in_thirds(ready, lambda to, dev: remote(gs_v.at[span], gb_v.at[chip, span], gs.at[g], gr.at[g], dev))

    def project(g, ready):
        pairs = GROUPS[g]
        n, at = len(pairs), pairs[0]

        @piece(ready)
        def _():
            whole_wait(gb_v.at[:, pl.ds(at, n)], gr.at[g])
            blocks = []
            for i in range(n):
                got = gb_v[:, at + i].astype(F32)
                blocks.append(jnp.concatenate([got[:, :8].reshape(128, 128), got[:, 8:].reshape(128, 128)], 1))
            rows = jnp.concatenate(blocks, 0).astype(BF16)
            terms = dot(rows, p2_v[...])
            for i, a in enumerate(group_slots(pairs)):
                cc_v[a] = rows[i * 64 : (i + 1) * 64]
                for m in range(3):
                    pr_v[a, m] = terms[i * 64 : (i + 1) * 64, m * 256 : (m + 1) * 256]

    conv(0, 8)
    conv(1, 16)
    reduce(0, 17)
    project(0, 22)
    conv(2, 24)
    reduce(1, 25)
    conv(3, 28)
    project(1, 29)
    reduce(2, 30)
    conv(4, 32)
    reduce(3, 32)
    project(2, 32)
    reduce(4, 32)
    project(3, 32)

    done = 0
    for step in range(1, 9):
        for hp, c in parts:
            if step <= 7 or hp == 0:
                to_right[step, hp, c].wait_recv()
                if step < 7 or (step == 7 and hp == 0):
                    pass_right(step + 1, hp, c)
            if step <= 7 or hp == 1:
                to_left[step, hp, c].wait_recv()
                if step < 7 or (step == 7 and hp == 1):
                    pass_left(step + 1, hp, c)
            done += 1
            for _ in range(2):
                if done < 32 and pieces and pieces[0][0] <= done:
                    pieces.pop(0)[1]()
    for _, f in pieces:
        f()

    sums_right = {}
    sums_left = {}

    def add_right(k, m):
        term = pr_v[slot_of(TO_RIGHT[m] - SHIFT[m] - k), m]
        if k:
            sums_right[k, m].wait_recv()
            term = rr_v[k - 1, m].astype(F32) + term
        sr_v[k, m] = term.astype(BF16)
        sums_right[k + 1, m] = remote(sr_v.at[k, m], rr_v.at[k, m], rs_s.at[0, k, m], rs_r.at[0, k, m], right)

    def add_left(k, m):
        term = pr_v[slot_of(k - (15 - TO_RIGHT[m]) - SHIFT[m]), m]
        if k:
            sums_left[k, m].wait_recv()
            term = rl_v[k - 1, m].astype(F32) + term
        sl_v[k, m] = term.astype(BF16)
        sums_left[k + 1, m] = remote(sl_v.at[k, m], rl_v.at[k, m], rs_s.at[1, k, m], rs_r.at[1, k, m], left)

    for m in ORDER:
        add_right(0, m)
    pieces.clear()
    project(4, 32)
    pieces.pop()[1]()
    for m in ORDER:
        add_left(0, m)

    offset = lax.rem(zt - z + NZ, NZ)
    place = jnp.where(offset == 0, 0, jnp.where(offset <= 8, 7 + offset, NZ - offset))

    @pl.when(zt != z)
    def _():
        remote(cc_v.at[place], r1_v, r1s.at[0], r1r.at[0], far)

    @pl.when(zt == z)
    def _():
        pltpu.make_async_copy(cc_v.at[place], r1_v, r1r.at[0]).start()

    for cp in fine_cp:
        cp.wait_send()
    whole_wait(wt_v.at[0, pl.ds(0, 7)], ws.at[0])
    pw_cp.wait_send()
    kept["wt"].wait_send()
    for hp in range(2):
        whole_wait(ts_v.at[hp, pl.ds(0, 7)], as_.at[hp])

    @pl.when(core != half)
    def _():
        for hp in range(2):
            whole_wait(ts_v.at[hp, 0], as_.at[2 + hp])

    for cp in list(to_right.values()) + list(to_left.values()):
        cp.wait_send()
    for g, pairs in enumerate(GROUPS):
        whole_wait(sb_v.at[pl.ds(0, 15), pl.ds(pairs[0], len(pairs))], ss.at[g])

    for k in range(1, 8):
        for m in ORDER:
            if k < TO_RIGHT[m]:
                add_right(k, m)
            if k < 15 - TO_RIGHT[m]:
                add_left(k, m)
        if k == 4:
            whole_wait(r1_v, r1r.at[0])

            @pl.when(z != 0)
            def _():
                remote(r1_v, res_v, r1s.at[1], r1r.at[1], res_chip)

            @pl.when(z == 0)
            def _():
                pltpu.make_async_copy(r1_v, res_v, r1r.at[1]).start()
            for g, pairs in enumerate(GROUPS):
                whole_wait(sb_v.at[pl.ds(0, 15), pl.ds(pairs[0], len(pairs))], gs.at[g])

    first = core == 0

    def exchange(i, both):
        f_v[i, core] = jnp.where(first, both[:, :128], both[:, 128:])
        xs_v[i] = jnp.where(first, both[:, 128:], both[:, :128])
        return remote(xs_v.at[i], f_v.at[i, core], xs.at[i], xr.at[i], sibling)

    whole_wait(res_v, r1r.at[1])
    swaps = [exchange(1, res_v[...])]
    kv_cp = []
    for m in ORDER:
        nr = TO_RIGHT[m]
        sums_right[nr, m].wait_recv()
        sums_left[15 - nr, m].wait_recv()
        both = pr_v[slot_of(-SHIFT[m]), m] + rr_v[nr - 1, m].astype(F32) + rl_v[14 - nr, m].astype(F32)
        both = both.astype(BF16)
        if m == 0:
            swaps.append(exchange(0, both))
            continue
        i = m - 1
        for c in range(2):
            ys_v[i, c] = both[:, c * 128 : (c + 1) * 128]
        kv_v[i, 1, core] = jnp.where(first, both[:, :128], both[:, 128:])
        for back, away in ((3, 2), (2, 1), (0, NZ - 1)):
            for c in range(2):
                kv_cp.append(
                    remote(
                        ys_v.at[i, c], kv_v.at[i, back, core], ks.at[i, back, c], kr.at[i, back, core], plane_at(away, c)
                    )
                )
        kv_cp.append(
            remote(ys_v.at[i, 1 - core], kv_v.at[i, 1, core], ks.at[i, 1, 0], kr.at[i, 1, core], sibling)
        )
    for cp in list(sums_right.values()) + list(sums_left.values()):
        cp.wait_send()

    @pl.when(zt != z)
    def _():
        whole_wait(r1_v, r1s.at[0])

    @pl.when(z != 0)
    def _():
        whole_wait(r1_v, r1s.at[1])

    for i in range(2):
        whole_wait(f_v.at[i, 1 - core], xr.at[i])
    for cp in swaps:
        cp.wait_send()
    for i in range(2):
        whole_wait(kv_v.at[i, 1, 1 - core], kr.at[i, 1, 1 - core])
        for back in (0, 2, 3):
            for c in range(2):
                whole_wait(kv_v.at[i, back, c], kr.at[i, back, c])

    q = f_v[0].reshape(128, 128)
    keys, vals = [[kv_v[i, back].reshape(128, 128) for back in range(4)] for i in range(2)]
    scores = []
    for back in range(4):
        seen = causal if back == 0 else z >= back
        scores.append(jnp.where(seen, dot_t(q, keys[back]) * SCALE, NEG))
    top = scores[0].max(1, keepdims=True)
    for back in range(1, 4):
        top = jnp.maximum(top, scores[back].max(1, keepdims=True))
    total = None
    mixed = None
    for back in range(4):
        e = jnp.exp(scores[back] - top)
        part_sum = jnp.sum(e, 1, keepdims=True)
        part_mix = dot(e.astype(BF16), vals[back])
        total = part_sum if total is None else total + part_sum
        mixed = part_mix if mixed is None else mixed + part_mix
    co_v[...] = (f_v[1].reshape(128, 128).astype(F32) + mixed / total).astype(BF16)
    co_cp = pltpu.make_async_copy(co_v, coarse_out.at[0], out_sem.at[1])
    co_cp.start()

    for cp in kv_cp:
        cp.wait_send()
    fo_cp.wait()
    co_cp.wait()


def per_device(fine_q, fine_k, fine_v, fine_x, conv_weight, qkv_weight):
    cw = conv_weight.transpose(0, 2, 1)
    pw = qkv_weight[0].transpose(1, 0, 2)
    dma = pltpu.SemaphoreType.DMA
    vmem = pltpu.VMEM
    scratch = [
        vmem((128, 512), BF16), vmem((128, 512), BF16), vmem((128, 512), BF16), vmem((128, 512), BF16),
        vmem((2, 128, 256), BF16), vmem((2, 128, 256), BF16),
        vmem((4, 128, 128), F32),
        vmem((128, 512), BF16),
        vmem((2, 8, 16, 256), BF16),
        vmem((16, 2, 2, 4, 16, 256), BF16),
        vmem((2, 8, 32, 512), BF16),
        vmem((2, 512, 256), BF16),
        vmem((2, 3, 256, 128), BF16),
        vmem((256, 768), BF16),
        vmem((16, 8, 16, 128), BF16),
        vmem((16, 8, 16, 128), BF16),
        vmem((8, 16, 128), BF16),
        vmem((16, 8, 16, 128), BF16),
        vmem((16, 64, 256), BF16),
        vmem((16, 3, 64, 256), F32),
        vmem((8, 3, 64, 256), BF16),
        vmem((8, 3, 64, 256), BF16),
        vmem((8, 3, 64, 256), BF16),
        vmem((8, 3, 64, 256), BF16),
        vmem((64, 256), BF16),
        vmem((64, 256), BF16),
        vmem((2, 64, 128), BF16),
        vmem((2, 2, 64, 128), BF16),
        vmem((2, 2, 64, 128), BF16),
        vmem((2, 4, 2, 64, 128), BF16),
        vmem((128, 128), BF16),
        dma((4,)), dma((4,)), dma((4,)), dma((3,)), dma((4,)), dma((4,)), dma((2,)),
        dma((2, 8, 2, 2)), dma((2, 8, 2, 2)),
        dma((5,)), dma((5,)), dma((5,)), dma((5,)),
        dma((2, 8, 3)), dma((2, 8, 3)),
        dma((2,)), dma((2,)), dma((2,)), dma((2,)),
        dma((2, 4, 2)), dma((2, 4, 2)), dma((2,)),
    ]
    return pl.pallas_call(
        kernel,
        out_shape=(
            jax.ShapeDtypeStruct((128, 512), BF16),
            jax.ShapeDtypeStruct((1, 128, 128), BF16),
        ),
        in_specs=[pl.BlockSpec(memory_space=pl.ANY)] * 6,
        out_specs=[pl.BlockSpec(memory_space=pl.ANY)] * 2,
        scratch_shapes=scratch,
        compiler_params=pltpu.CompilerParams(
            collective_id=0, has_side_effects=True, vmem_limit_bytes=60 * 1024 * 1024
        ),
    )(fine_q, fine_k, fine_v, fine_x, cw, pw)


def solution(mesh):
    placed = (
        P("ctx", "head"),
        P("ctx", "head"),
        P("ctx", "head"),
        P("ctx", "head"),
        P(None, "head", "ctx"),
        P("ctx", None, None, "head"),
    )
    return jax.shard_map(
        per_device,
        mesh=mesh,
        in_specs=placed,
        out_specs=(P("ctx", "head"), P("ctx", None, "head")),
        check_vma=False,
    )
```

time: 117 us -> 114 us (0.974); the launches traced: 116 us -> 114 us
  Pallas kernels: 113 us -> 111 us
    pallas_call x1, Pallas kernels: 113 us -> 111 us  [per_device(): pl.pallas_call(kernel, out_shape=(jax.ShapeDtypeStruct((128, 512), BF16),...]
where the time goes in v2:
time: 114 us
  Pallas kernels  111 us (97%)
  local copies, waits for them, and re-layouts  2.19 us (2%)
    pallas_call x1, Pallas kernels, per_device(): pl.pallas_call(kernel, out_shape=(jax.ShapeDtypeStruct((128, 512), BF16),...  111 us

profile of v2, /device:TPU:1, one launch (start us, length us, event | category | flops | bytes accessed | tf_op | source)
XLA Modules:
  0.0 114.0 jit_solution(3752065031144248540)
XLA Ops:
  0.6 111.2 %shard_map.77 = (bf16[128,512]{1,0:T(8,128)(2,1)}, bf16[1,128,128]{2,1,0:T(8,128)(2,1)}) custom-call(bf16[128,512]{1,0:T(8,128)(2,1)} %q_in.1, bf16[128,512]{1,0:T(8,128)(2,1)} %k_in.1, bf16[128,512]{1,0:T(8,128)(2,1)} %v_in.1, bf16[128,512]{1,0:T(8,128)(2,1)} %x_in.1, bf16[8,32,512]{2,1,0:T(8,128)(2,1)} %bitcast.4, bf16[3,256,128]{2,1,0:T(8,128)(2,1)} %bitcast.5), custom_call_target="tpu_custom_call" | custom-call | tf_op jit(solution)/shard_map/pallas_call | solution.py:528
  111.8 0.0 copy-start
  111.8 1.6 %copy.10 = bf16[128,512]{1,0:T(8,128)(2,1)} copy(bf16[128,512]{1,0:T(8,128)(2,1)} %get-tuple-element.4) | data formatting | bytes 262144
  113.4 0.0 copy-done
  113.4 0.6 copy.11
Async XLA Ops:
  111.8 1.6 %copy-start = (bf16[1,128,128]{2,1,0:T(8,128)(2,1)S(1)}, bf16[1,128,128]{2,1,0:T(8,128)(2,1)}, u32[]{:S(2)}) copy-start(bf16[1,128,128]{2,1,0:T(8,128)(2,1)} %get-tuple-element.5) | copy-start | bytes 98308

commit v3 on v2

v3 whole, which is shorter than its diff:
```python
import jax
import jax.numpy as jnp
from jax import lax
from jax.experimental import pallas as pl
from jax.experimental.pallas import tpu as pltpu
from jax.sharding import PartitionSpec as P

STRIDE = 8
HEAD_DIM = 128
NZ = 16
MESH = pl.DeviceIdType.MESH
BF16 = jnp.bfloat16
F32 = jnp.float32
SCALE = HEAD_DIM ** -0.5
NEG = -1e30
GROUPS = 4
TO_RIGHT = (7, 8, 8)
SHIFT = (0, 1, 1)
ORDER = (1, 2, 0)


def slot_of(offset):
    if offset == -8:
        offset = 8
    return -offset if offset <= 0 else 7 + offset


def dot_t(a, b):
    return lax.dot_general(a, b, (((1,), (1,)), ((), ())), preferred_element_type=F32)


def dot(a, b):
    return jnp.dot(a, b, preferred_element_type=F32)


def whole_wait(ref, sem):
    pltpu.make_async_copy(ref, ref, sem).wait()


def kernel(
    q_in, k_in, v_in, x_in, cw_in, pw_in, fine_out, coarse_out,
    q_v, k_v, v_v, x_v, pk_v, pv_v, mix_v, st_v, fo_v, ts_v, acts, wt_v, w2_v, pw_v, p2_v,
    sb_v, rb_v, gs_v, gb_v, cc_v, pr_v, rr_v, rl_v, sr_v, sl_v, r1_v, res_v, xs_v, f_v, ys_v, kv_v, co_v,
    in_sem, fs, fr, ws, wr, as_, ar, zs, zr, ss, sr, gs, gr, rs_s, rs_r, r1s, r1r, xs, xr, ks, kr, out_sem,
):
    ctx = lax.axis_index("ctx")
    head = lax.axis_index("head")
    z = lax.div(ctx, 8)
    s = lax.rem(ctx, 8)
    yl = lax.div(head, 2)
    core = lax.rem(head, 2)
    chip = 2 * s + yl
    half = lax.div(s, 4)
    quarter = lax.rem(s, 4)
    sibling = (ctx, 2 * yl + 1 - core)
    after = (lax.rem(ctx + 1, 128), head)
    before = (lax.rem(ctx + 127, 128), head)
    right = (lax.rem(z + 1, NZ) * 8 + s, head)
    left = (lax.rem(z + NZ - 1, NZ) * 8 + s, head)
    zt = lax.rem(chip - z + NZ, NZ)
    far = (zt * 8 + s, head)

    def chip_at(c):
        return (z * 8 + lax.div(c, 2), lax.rem(c, 2) * 2 + core)

    def loop(low, high, body):
        def step(i, carry):
            body(i)
            return carry

        lax.fori_loop(low, high, step, 0)


    def plane_at(away, c):
        return (lax.rem(z + away, NZ) * 8 + s, 2 * yl + c)

    def remote(src, dst, send, recv, dev):
        cp = pltpu.make_async_remote_copy(
            src_ref=src, dst_ref=dst, send_sem=send, recv_sem=recv, device_id=dev, device_id_type=MESH
        )
        cp.start()
        return cp

    loads = []
    for i, (src, dst) in enumerate([(q_in, q_v), (k_in, k_v), (v_in, v_v), (x_in, x_v)]):
        cp = pltpu.make_async_copy(src, dst, in_sem.at[i])
        cp.start()
        loads.append(cp)

    barrier = pltpu.get_barrier_semaphore()

    def greet(dev):
        pl.semaphore_signal(barrier, inc=1, device_id=dev, device_id_type=MESH)

    for dev in (after, before):
        greet(dev)
    for away in (1, 2, NZ - 2, NZ - 1):
        for c in range(2):
            greet(plane_at(away, c))

    loop(1, 16, lambda j: greet(chip_at(lax.rem(chip + j, 16))))
    loop(0, 8, lambda j: greet((z * 8 + j, 2 * yl + 1 - core)))

    @pl.when(zt != z)
    def _():
        greet(far)

    pl.semaphore_wait(barrier, 33 + jnp.where(zt != z, 1, 0))

    fine_cp = []
    for hp in range(2):
        cols = pl.ds(hp * 256, 256)
        for i, (src, dst) in enumerate([(k_in, pk_v), (v_in, pv_v)]):
            fine_cp.append(remote(src.at[:, cols], dst.at[hp], fs.at[2 * hp + i], fr.at[2 * hp + i], after))

    row = lax.broadcasted_iota(jnp.int32, (128, 128), 0)
    col = lax.broadcasted_iota(jnp.int32, (128, 128), 1)
    causal = col <= row
    for cp in loads:
        cp.wait()

    def own_part(hp):
        for j in range(2):
            i = 2 * hp + j
            cols = pl.ds(pl.multiple_of(i * 128, 128), 128)
            scores = jnp.where(causal, dot_t(q_v[:, cols], k_v[:, cols]) * SCALE, NEG)
            top = jnp.max(scores, 1, keepdims=True)
            e = jnp.exp(scores - top)
            mix_v[i] = dot(e.astype(BF16), v_v[:, cols])
            st_v[i, 0] = top
            st_v[i, 1] = jnp.sum(e, 1, keepdims=True)

    loop(0, 2, own_part)
    has_before = ctx > 0

    def whole_part(hp):
        whole_wait(pk_v.at[hp], fr.at[2 * hp])
        whole_wait(pv_v.at[hp], fr.at[2 * hp + 1])
        for j in range(2):
            i = 2 * hp + j
            cols = pl.ds(pl.multiple_of(i * 128, 128), 128)
            near = slice(j * 128, (j + 1) * 128)
            scores = jnp.where(has_before, dot_t(q_v[:, cols], pk_v[hp, :, near]) * SCALE, NEG)
            own_top, own_sum = st_v[i, 0], st_v[i, 1]
            top = jnp.maximum(own_top, jnp.max(scores, 1, keepdims=True))
            scale = jnp.exp(own_top - top)
            e = jnp.exp(scores - top)
            total = own_sum * scale + jnp.sum(e, 1, keepdims=True)
            mixed = mix_v[i] * scale + dot(e.astype(BF16), pv_v[hp, :, near])
            result = x_v[:, cols].astype(F32) + mixed / total
            mix_v[i] = result
            fo_v[:, cols] = result.astype(BF16)
            for tap in range(8):
                ts_v[hp, tap, :, near] = mix_v[i, pl.ds(tap, 16, stride=8), :].astype(BF16)

        def send(j):
            to = lax.rem(s + j, 8)
            remote(
                ts_v.at[hp, to], acts.at[0, hp, core, quarter], as_.at[hp], ar.at[hp], (z * 8 + to, 2 * yl + half)
            )

        loop(1, 8, send)

        @pl.when(core == half)
        def _():
            pltpu.make_async_copy(ts_v.at[hp, s], acts.at[0, hp, core, quarter], ar.at[hp]).start()

        @pl.when(core != half)
        def _():
            remote(ts_v.at[hp, s], acts.at[0, hp, core, quarter], as_.at[2 + hp], ar.at[hp], sibling)

    loop(0, 2, whole_part)

    parts = [(hp, c) for hp in range(2) for c in range(2)]

    def place_right(k):
        return jnp.where(k == 8, 15, k)

    def place_left(k):
        return jnp.where(k == 0, 0, 7 + k)

    def pass_right(k, hp, c):
        remote(
            acts.at[place_right(k - 1), hp, c], acts.at[place_right(k), hp, c],
            zs.at[0, k - 1, hp, c], zr.at[0, k - 1, hp, c], right,
        )

    def pass_left(k, hp, c):
        remote(
            acts.at[place_left(k - 1), hp, c], acts.at[place_left(k), hp, c],
            zs.at[1, k - 1, hp, c], zr.at[1, k - 1, hp, c], left,
        )

    def got_right(k, hp, c):
        whole_wait(acts.at[place_right(k), hp, c], zr.at[0, k - 1, hp, c])

    def got_left(k, hp, c):
        whole_wait(acts.at[place_left(k), hp, c], zr.at[1, k - 1, hp, c])

    for hp in range(2):
        whole_wait(acts.at[0, hp], ar.at[hp])
        for c in range(2):
            pass_right(1, hp, c)
            pass_left(1, hp, c)

    def send_weights(j):
        to = lax.rem(s + j, 8)
        remote(cw_in.at[to], wt_v.at[core, s], ws.at[0], wr.at[0], (z * 8 + to, head))

    loop(1, 8, send_weights)
    pltpu.make_async_copy(cw_in.at[s], wt_v.at[core, s], wr.at[0]).start()
    pw_cp = remote(pw_in, pw_v.at[core], ws.at[1], wr.at[1], sibling)
    pw_own = pltpu.make_async_copy(pw_in, pw_v.at[core], wr.at[2])
    pw_own.start()
    fo_cp = pltpu.make_async_copy(fo_v, fine_out, out_sem.at[0])
    fo_cp.start()

    def turn(c):
        def part(hp):
            cols = pl.ds(pl.multiple_of(hp * 256, 256), 256)
            w2_v[c, cols, :] = wt_v[c, :, :, cols].reshape(256, 256).T

        loop(0, 2, part)

    def group_slots(g):
        return [2 * g, 2 * g + 8, 2 * g + 1, 2 * g + 9]

    def conv(g):
        total = None
        for hp, c in parts:
            rows = jnp.concatenate([acts[a, hp, c].reshape(64, 256) for a in group_slots(g)], 0)
            term = dot(rows, w2_v[c, hp * 256 : (hp + 1) * 256, :])
            total = term if total is None else total + term
        for i in range(2):
            lo = total[i * 128 : (i + 1) * 128, :128].reshape(16, 8, 128)
            hi = total[i * 128 : (i + 1) * 128, 128:].reshape(16, 8, 128)
            sb_v[g, :, i] = jnp.concatenate([lo, hi], 1).astype(BF16)

        def send(j):
            to = lax.rem(chip + j, 16)
            remote(sb_v.at[g, to], rb_v.at[g, chip], ss.at[g], sr.at[g], chip_at(to))

        loop(1, 16, send)
        pltpu.make_async_copy(sb_v.at[g, chip], rb_v.at[g, chip], sr.at[g]).start()

    def reduce(g):
        whole_wait(rb_v.at[g], sr.at[g])
        gs_v[g] = jnp.sum(rb_v[g].astype(F32), 0).astype(BF16)

        def send(j):
            remote(gs_v.at[g], gb_v.at[g, chip], gs.at[g], gr.at[g], chip_at(lax.rem(chip + j, 16)))

        loop(1, 16, send)
        pltpu.make_async_copy(gs_v.at[g], gb_v.at[g, chip], gr.at[g]).start()

    def project(g):
        whole_wait(gb_v.at[g], gr.at[g])
        blocks = []
        for i in range(2):
            got = gb_v[g, :, i].astype(F32)
            blocks.append(jnp.concatenate([got[:, :8].reshape(128, 128), got[:, 8:].reshape(128, 128)], 1))
        rows = jnp.concatenate(blocks, 0).astype(BF16)
        for i, a in enumerate(group_slots(g)):
            cc_v[a] = rows[i * 64 : (i + 1) * 64]

        def one(m):
            terms = dot(rows, p2_v[m])
            for i, a in enumerate(group_slots(g)):
                pr_v[a, m] = terms[i * 64 : (i + 1) * 64]

        for m in range(3):
            one(m)

    def turn_of(i):
        more = i < GROUPS - 1

        def odd(parts):
            k = 2 * i + 1
            for hp, c in parts:
                got_right(k, hp, c)
                got_left(k, hp, c)
                if hp == 0:
                    pass_right(k + 1, hp, c)
                    pl.when(more)(lambda: pass_left(k + 1, hp, c))
                else:
                    pass_left(k + 1, hp, c)
                    pl.when(more)(lambda: pass_right(k + 1, hp, c))

        def even(parts):
            k = 2 * i + 2
            for hp, c in parts:
                if hp == 0:
                    got_right(k, hp, c)
                else:
                    got_left(k, hp, c)

                @pl.when(more)
                def _():
                    if hp == 0:
                        got_left(k, hp, c)
                    else:
                        got_right(k, hp, c)
                    pass_right(k + 1, hp, c)
                    pass_left(k + 1, hp, c)

        ringing = pl.when(i < GROUPS)
        ringing(lambda: odd(parts[:2]))

        @pl.when(i == 0)
        def _():
            whole_wait(wt_v.at[core], wr.at[0])
            remote(wt_v.at[core], wt_v.at[core], ws.at[2], wr.at[3], sibling)
            pw_own.wait()
            whole_wait(pw_v.at[1 - core], wr.at[1])
            for m in range(3):
                for part in range(2):
                    p2_v[m, :, part * 128 : (part + 1) * 128] = pw_v[part, m]

        pl.when(i >= 2)(lambda: project(i - 2))
        ringing(lambda: odd(parts[2:]))
        pl.when(i == 0)(lambda: turn(core))
        pl.when((i >= 1) & (i <= GROUPS))(lambda: reduce(i - 1))
        ringing(lambda: even(parts))

        @pl.when(i == 0)
        def _():
            whole_wait(wt_v.at[1 - core], wr.at[3])
            turn(1 - core)

        ringing(lambda: conv(i))

    loop(0, GROUPS + 2, turn_of)

    def place_of(offset):
        return jnp.where(offset <= 0, -offset, 7 + offset)

    def add_right(k, m):
        whole_wait(rr_v.at[k - 1, m], rs_r.at[0, k - 1, m])
        term = rr_v[k - 1, m].astype(F32) + pr_v[place_of(TO_RIGHT[m] - SHIFT[m] - k), m]
        sr_v[k, m] = term.astype(BF16)
        remote(sr_v.at[k, m], rr_v.at[k, m], rs_s.at[0, k, m], rs_r.at[0, k, m], right)

    def add_left(k, m):
        whole_wait(rl_v.at[k - 1, m], rs_r.at[1, k - 1, m])
        term = rl_v[k - 1, m].astype(F32) + pr_v[place_of(k - (15 - TO_RIGHT[m]) - SHIFT[m]), m]
        sl_v[k, m] = term.astype(BF16)
        remote(sl_v.at[k, m], rl_v.at[k, m], rs_s.at[1, k, m], rs_r.at[1, k, m], left)

    for m in ORDER:
        sr_v[0, m] = pr_v[slot_of(7), m].astype(BF16)
        remote(sr_v.at[0, m], rr_v.at[0, m], rs_s.at[0, 0, m], rs_r.at[0, 0, m], right)
        sl_v[0, m] = pr_v[slot_of(8), m].astype(BF16)
        remote(sl_v.at[0, m], rl_v.at[0, m], rs_s.at[1, 0, m], rs_r.at[1, 0, m], left)

    offset = lax.rem(zt - z + NZ, NZ)
    place = jnp.where(offset == 0, 0, jnp.where(offset <= 8, 7 + offset, NZ - offset))

    @pl.when(zt != z)
    def _():
        remote(cc_v.at[place], r1_v, r1s.at[0], r1r.at[0], far)

    @pl.when(zt == z)
    def _():
        pltpu.make_async_copy(cc_v.at[place], r1_v, r1r.at[0]).start()

    for i in range(4):
        whole_wait(pk_v.at[0], fs.at[i])
    whole_wait(wt_v.at[0, pl.ds(0, 7)], ws.at[0])
    pw_cp.wait_send()
    whole_wait(wt_v.at[0], ws.at[2])
    for hp in range(2):
        whole_wait(ts_v.at[hp, pl.ds(0, 7)], as_.at[hp])

    @pl.when(core != half)
    def _():
        for hp in range(2):
            whole_wait(ts_v.at[hp, 0], as_.at[2 + hp])

    def ring_left(k):
        for c in range(2):
            for way in range(2):
                whole_wait(acts.at[0, 0, c], zs.at[way, k, way, c])
                pl.when(k < 7)(lambda: whole_wait(acts.at[0, 0, c], zs.at[way, k, 1 - way, c]))

    loop(0, 8, ring_left)
    loop(0, GROUPS, lambda g: whole_wait(sb_v.at[g, pl.ds(0, 15)], ss.at[g]))

    def sums(k):
        for m in ORDER:
            add_right(k, m)
            add_left(k, m)

        @pl.when(k == 4)
        def _():
            whole_wait(r1_v, r1r.at[0])

            @pl.when(z != 0)
            def _():
                remote(r1_v, res_v, r1s.at[1], r1r.at[1], chip_at(zt))

            @pl.when(z == 0)
            def _():
                pltpu.make_async_copy(r1_v, res_v, r1r.at[1]).start()

    loop(1, 7, sums)
    loop(0, GROUPS, lambda g: whole_wait(sb_v.at[g, pl.ds(0, 15)], gs.at[g]))
    for m in ORDER:
        if TO_RIGHT[m] == 8:
            add_right(7, m)
        else:
            add_left(7, m)

    first = core == 0

    def exchange(i, both):
        f_v[i, core] = jnp.where(first, both[:, :128], both[:, 128:])
        xs_v[i] = jnp.where(first, both[:, 128:], both[:, :128])
        return remote(xs_v.at[i], f_v.at[i, core], xs.at[i], xr.at[i], sibling)

    whole_wait(res_v, r1r.at[1])
    swaps = [exchange(1, res_v[...])]
    kv_cp = []
    for m in ORDER:
        nr = TO_RIGHT[m]
        whole_wait(rr_v.at[nr - 1, m], rs_r.at[0, nr - 1, m])
        whole_wait(rl_v.at[14 - nr, m], rs_r.at[1, 14 - nr, m])
        both = pr_v[slot_of(-SHIFT[m]), m] + rr_v[nr - 1, m].astype(F32) + rl_v[14 - nr, m].astype(F32)
        both = both.astype(BF16)
        if m == 0:
            swaps.append(exchange(0, both))
            continue
        i = m - 1
        for c in range(2):
            ys_v[i, c] = both[:, c * 128 : (c + 1) * 128]
        kv_v[i, 1, core] = jnp.where(first, both[:, :128], both[:, 128:])
        for back, away in ((3, 2), (2, 1), (0, NZ - 1)):
            for c in range(2):
                kv_cp.append(
                    remote(
                        ys_v.at[i, c], kv_v.at[i, back, core], ks.at[i, back, c], kr.at[i, back, core], plane_at(away, c)
                    )
                )
        kv_cp.append(
            remote(ys_v.at[i, 1 - core], kv_v.at[i, 1, core], ks.at[i, 1, 0], kr.at[i, 1, core], sibling)
        )
    def sums_left(k):
        for m in ORDER:
            for way in range(2):
                whole_wait(sr_v.at[0, m], rs_s.at[way, k, m])

    loop(0, 7, sums_left)
    for m in ORDER:
        whole_wait(sr_v.at[0, m], rs_s.at[0 if TO_RIGHT[m] == 8 else 1, 7, m])

    @pl.when(zt != z)
    def _():
        whole_wait(r1_v, r1s.at[0])

    @pl.when(z != 0)
    def _():
        whole_wait(r1_v, r1s.at[1])

    for i in range(2):
        whole_wait(f_v.at[i, 1 - core], xr.at[i])
    for cp in swaps:
        cp.wait_send()
    for i in range(2):
        whole_wait(kv_v.at[i, 1, 1 - core], kr.at[i, 1, 1 - core])
        for back in (0, 2, 3):
            for c in range(2):
                whole_wait(kv_v.at[i, back, c], kr.at[i, back, c])

    q = f_v[0].reshape(128, 128)
    keys, vals = [[kv_v[i, back].reshape(128, 128) for back in range(4)] for i in range(2)]
    scores = []
    for back in range(4):
        seen = causal if back == 0 else z >= back
        scores.append(jnp.where(seen, dot_t(q, keys[back]) * SCALE, NEG))
    top = scores[0].max(1, keepdims=True)
    for back in range(1, 4):
        top = jnp.maximum(top, scores[back].max(1, keepdims=True))
    total = None
    mixed = None
    for back in range(4):
        e = jnp.exp(scores[back] - top)
        part_sum = jnp.sum(e, 1, keepdims=True)
        part_mix = dot(e.astype(BF16), vals[back])
        total = part_sum if total is None else total + part_sum
        mixed = part_mix if mixed is None else mixed + part_mix
    co_v[...] = (f_v[1].reshape(128, 128).astype(F32) + mixed / total).astype(BF16)
    co_cp = pltpu.make_async_copy(co_v, coarse_out.at[0], out_sem.at[1])
    co_cp.start()

    for cp in kv_cp:
        cp.wait_send()
    fo_cp.wait()
    co_cp.wait()


def per_device(fine_q, fine_k, fine_v, fine_x, conv_weight, qkv_weight):
    cw = conv_weight.transpose(0, 2, 1)
    pw = qkv_weight[0].transpose(1, 0, 2)
    dma = pltpu.SemaphoreType.DMA
    vmem = pltpu.VMEM
    scratch = [
        vmem((128, 512), BF16), vmem((128, 512), BF16), vmem((128, 512), BF16), vmem((128, 512), BF16),
        vmem((2, 128, 256), BF16), vmem((2, 128, 256), BF16),
        vmem((4, 128, 128), F32),
        vmem((4, 2, 128, 1), F32),
        vmem((128, 512), BF16),
        vmem((2, 8, 16, 256), BF16),
        vmem((16, 2, 2, 4, 16, 256), BF16),
        vmem((2, 8, 32, 512), BF16),
        vmem((2, 512, 256), BF16),
        vmem((2, 3, 256, 128), BF16),
        vmem((3, 256, 256), BF16),
        vmem((4, 16, 2, 16, 128), BF16),
        vmem((4, 16, 2, 16, 128), BF16),
        vmem((4, 2, 16, 128), BF16),
        vmem((4, 16, 2, 16, 128), BF16),
        vmem((16, 64, 256), BF16),
        vmem((16, 3, 64, 256), F32),
        vmem((8, 3, 64, 256), BF16),
        vmem((8, 3, 64, 256), BF16),
        vmem((8, 3, 64, 256), BF16),
        vmem((8, 3, 64, 256), BF16),
        vmem((64, 256), BF16),
        vmem((64, 256), BF16),
        vmem((2, 64, 128), BF16),
        vmem((2, 2, 64, 128), BF16),
        vmem((2, 2, 64, 128), BF16),
        vmem((2, 4, 2, 64, 128), BF16),
        vmem((128, 128), BF16),
        dma((4,)), dma((4,)), dma((4,)), dma((3,)), dma((4,)), dma((4,)), dma((2,)),
        dma((2, 8, 2, 2)), dma((2, 8, 2, 2)),
        dma((4,)), dma((4,)), dma((4,)), dma((4,)),
        dma((2, 8, 3)), dma((2, 8, 3)),
        dma((2,)), dma((2,)), dma((2,)), dma((2,)),
        dma((2, 4, 2)), dma((2, 4, 2)), dma((2,)),
    ]
    return pl.pallas_call(
        kernel,
        out_shape=(
            jax.ShapeDtypeStruct((128, 512), BF16),
            jax.ShapeDtypeStruct((1, 128, 128), BF16),
        ),
        in_specs=[pl.BlockSpec(memory_space=pl.ANY)] * 6,
        out_specs=[pl.BlockSpec(memory_space=pl.ANY)] * 2,
        scratch_shapes=scratch,
        compiler_params=pltpu.CompilerParams(
            collective_id=0, has_side_effects=True, vmem_limit_bytes=60 * 1024 * 1024
        ),
    )(fine_q, fine_k, fine_v, fine_x, cw, pw)


def solution(mesh):
    placed = (
        P("ctx", "head"),
        P("ctx", "head"),
        P("ctx", "head"),
        P("ctx", "head"),
        P(None, "head", "ctx"),
        P("ctx", None, None, "head"),
    )
    return jax.shard_map(
        per_device,
        mesh=mesh,
        in_specs=placed,
        out_specs=(P("ctx", "head"), P("ctx", None, "head")),
        check_vma=False,
    )
```

time: 114 us -> 114 us (level)
  no operation moved by 1% of the time
where the time goes in v3:
time: 114 us; the launch traced here: 113 us
  Pallas kernels  111 us (97%)
  local copies, waits for them, and re-layouts  2.19 us (2%)
    pallas_call x1, Pallas kernels, per_device(): pl.pallas_call(kernel, out_shape=(jax.ShapeDtypeStruct((128, 512), BF16),...  111 us

profile of v3, /device:TPU:1, one launch (start us, length us, event | category | flops | bytes accessed | tf_op | source)
XLA Modules:
  0.0 113.4 jit_solution(4562744396688524372)
XLA Ops:
  0.6 110.6 %shard_map.77 = (bf16[128,512]{1,0:T(8,128)(2,1)}, bf16[1,128,128]{2,1,0:T(8,128)(2,1)}) custom-call(bf16[128,512]{1,0:T(8,128)(2,1)} %q_in.1, bf16[128,512]{1,0:T(8,128)(2,1)} %k_in.1, bf16[128,512]{1,0:T(8,128)(2,1)} %v_in.1, bf16[128,512]{1,0:T(8,128)(2,1)} %x_in.1, bf16[8,32,512]{2,1,0:T(8,128)(2,1)} %bitcast.4, bf16[3,256,128]{2,1,0:T(8,128)(2,1)} %bitcast.5), custom_call_target="tpu_custom_call" | custom-call | tf_op jit(solution)/shard_map/pallas_call | solution.py:541
  111.2 0.0 copy-start
  111.3 1.6 %copy.10 = bf16[128,512]{1,0:T(8,128)(2,1)} copy(bf16[128,512]{1,0:T(8,128)(2,1)} %get-tuple-element.4) | data formatting | bytes 262144
  112.8 0.0 copy-done
  112.8 0.6 copy.11
Async XLA Ops:
  111.2 1.6 %copy-start = (bf16[1,128,128]{2,1,0:T(8,128)(2,1)S(1)}, bf16[1,128,128]{2,1,0:T(8,128)(2,1)}, u32[]{:S(2)}) copy-start(bf16[1,128,128]{2,1,0:T(8,128)(2,1)} %get-tuple-element.5) | copy-start | bytes 98308

commit v4 on v3

--- a/solution.py
+++ b/solution.py
@@ -14,8 +14,6 @@
 SCALE = HEAD_DIM ** -0.5
 NEG = -1e30
 GROUPS = 4
-TO_RIGHT = (7, 8, 8)
-SHIFT = (0, 1, 1)
 ORDER = (1, 2, 0)
 
 
@@ -39,9 +37,9 @@
 
 def kernel(
     q_in, k_in, v_in, x_in, cw_in, pw_in, fine_out, coarse_out,
-    q_v, k_v, v_v, x_v, pk_v, pv_v, mix_v, st_v, fo_v, ts_v, acts, wt_v, w2_v, pw_v, p2_v,
-    sb_v, rb_v, gs_v, gb_v, cc_v, pr_v, rr_v, rl_v, sr_v, sl_v, r1_v, res_v, xs_v, f_v, ys_v, kv_v, co_v,
-    in_sem, fs, fr, ws, wr, as_, ar, zs, zr, ss, sr, gs, gr, rs_s, rs_r, r1s, r1r, xs, xr, ks, kr, out_sem,
+    q_v, k_v, v_v, x_v, pk_v, pv_v, mix_v, st_v, fo_v, ts_v, acts, wt_v, w2_v, pw_v,
+    sb_v, rb_v, gs_v, gt_v, gb_v, cc_v, acc_v, xs_v, f_v, ys_v, kv_v, co_v,
+    in_sem, fs, fr, ws, wr, as_, ar, zs, zr, ss, sr, gs, gr, hs, hr, wzs, wzr, wss, wsr, xs, xr, ks, kr, out_sem,
 ):
     ctx = lax.axis_index("ctx")
     head = lax.axis_index("head")
@@ -57,8 +55,6 @@
     before = (lax.rem(ctx + 127, 128), head)
     right = (lax.rem(z + 1, NZ) * 8 + s, head)
     left = (lax.rem(z + NZ - 1, NZ) * 8 + s, head)
-    zt = lax.rem(chip - z + NZ, NZ)
-    far = (zt * 8 + s, head)
 
     def chip_at(c):
         return (z * 8 + lax.div(c, 2), lax.rem(c, 2) * 2 + core)
@@ -94,24 +90,51 @@
 
     for dev in (after, before):
         greet(dev)
-    for away in (1, 2, NZ - 2, NZ - 1):
-        for c in range(2):
-            greet(plane_at(away, c))
-
+    loop(1, NZ, lambda j: greet(plane_at(j, core)))
+    for away in (1, 2, 3, NZ - 3, NZ - 2, NZ - 1):
+        greet(plane_at(away, 1 - core))
     loop(1, 16, lambda j: greet(chip_at(lax.rem(chip + j, 16))))
     loop(0, 8, lambda j: greet((z * 8 + j, 2 * yl + 1 - core)))
 
-    @pl.when(zt != z)
-    def _():
-        greet(far)
-
-    pl.semaphore_wait(barrier, 33 + jnp.where(zt != z, 1, 0))
+    pl.semaphore_wait(barrier, 46)
 
     fine_cp = []
     for hp in range(2):
         cols = pl.ds(hp * 256, 256)
         for i, (src, dst) in enumerate([(k_in, pk_v), (v_in, pv_v)]):
             fine_cp.append(remote(src.at[:, cols], dst.at[hp], fs.at[2 * hp + i], fr.at[2 * hp + i], after))
+
+    lanes = pl.ds(pl.multiple_of(core * 128, 128), 128)
+    other_lanes = pl.ds(pl.multiple_of((1 - core) * 128, 128), 128)
+
+    def held(slot):
+        return pw_v.at[slot, :, :, lanes]
+
+    pw_own = pltpu.make_async_copy(pw_in, held(0), wr.at[2])
+    pw_own.start()
+    remote(pw_in, held(1), wzs.at[0, 0], wzr.at[0, 0], right)
+    remote(pw_in, held(8), wzs.at[1, 0], wzr.at[1, 0], left)
+    remote(pw_in, held(0), wss.at[0], wsr.at[0], sibling)
+
+    def weights_step(k, on=True):
+        whole_wait(held(k), wzr.at[0, k - 1])
+        if on:
+            remote(held(k), held(k + 1), wzs.at[0, k], wzr.at[0, k], right)
+        else:
+            remote(pw_v.at[7, 2, :, lanes], pw_v.at[15, 2, :, lanes], wzs.at[0, 7], wzr.at[0, 7], right)
+        whole_wait(held(7 + k), wzr.at[1, k - 1])
+        if on:
+            remote(held(7 + k), held(8 + k), wzs.at[1, k], wzr.at[1, k], left)
+        else:
+            two = pl.ds(0, 2)
+            remote(pw_v.at[14, two, :, lanes], pw_v.at[15, two, :, lanes], wzs.at[1, 7], wzr.at[1, 7], left)
+        remote(held(k), held(k), wss.at[k], wsr.at[k], sibling)
+        remote(held(7 + k), held(7 + k), wss.at[7 + k], wsr.at[7 + k], sibling)
+
+    def weights_end():
+        whole_wait(pw_v.at[15, 2, :, lanes], wzr.at[0, 7])
+        whole_wait(pw_v.at[15, pl.ds(0, 2), :, lanes], wzr.at[1, 7])
+        remote(held(15), held(15), wss.at[15], wsr.at[15], sibling)
 
     row = lax.broadcasted_iota(jnp.int32, (128, 128), 0)
     col = lax.broadcasted_iota(jnp.int32, (128, 128), 1)
@@ -169,6 +192,8 @@
         def _():
             remote(ts_v.at[hp, s], acts.at[0, hp, core, quarter], as_.at[2 + hp], ar.at[hp], sibling)
 
+        pl.when(hp == 0)(lambda: weights_step(1))
+
     loop(0, 2, whole_part)
 
     parts = [(hp, c) for hp in range(2) for c in range(2)]
@@ -209,9 +234,7 @@
 
     loop(1, 8, send_weights)
     pltpu.make_async_copy(cw_in.at[s], wt_v.at[core, s], wr.at[0]).start()
-    pw_cp = remote(pw_in, pw_v.at[core], ws.at[1], wr.at[1], sibling)
-    pw_own = pltpu.make_async_copy(pw_in, pw_v.at[core], wr.at[2])
-    pw_own.start()
+    weights_step(2)
     fo_cp = pltpu.make_async_copy(fo_v, fine_out, out_sem.at[0])
     fo_cp.start()
 
@@ -247,29 +270,49 @@
         whole_wait(rb_v.at[g], sr.at[g])
         gs_v[g] = jnp.sum(rb_v[g].astype(F32), 0).astype(BF16)
 
+        for i in range(2):
+            p = 2 * g + i
+            away = jnp.where(chip < 8, lax.rem(NZ - p, NZ), p + 1)
+
+            @pl.when(away != 0)
+            def _():
+                remote(gs_v.at[g, i], gt_v.at[g, i], hs.at[g, i], hr.at[g, i], plane_at(away, core))
+
+            @pl.when(away == 0)
+            def _():
+                pltpu.make_async_copy(gs_v.at[g, i], gt_v.at[g, i], hr.at[g, i]).start()
+
+    def spread(g):
+        for i in range(2):
+            whole_wait(gt_v.at[g, i], hr.at[g, i])
+
         def send(j):
-            remote(gs_v.at[g], gb_v.at[g, chip], gs.at[g], gr.at[g], chip_at(lax.rem(chip + j, 16)))
+            remote(gt_v.at[g], gb_v.at[g, chip], gs.at[g], gr.at[g], chip_at(lax.rem(chip + j, 16)))
 
         loop(1, 16, send)
-        pltpu.make_async_copy(gs_v.at[g], gb_v.at[g, chip], gr.at[g]).start()
+        pltpu.make_async_copy(gt_v.at[g], gb_v.at[g, chip], gr.at[g]).start()
+
+    def weight_slots(g):
+        return [jnp.where(g == 0, 0, 7 + 2 * g), 8 + 2 * g, 2 * g + 1, jnp.where(g == 3, 15, 2 * g + 2)]
 
     def project(g):
+        slots = weight_slots(g)
+        for slot in slots:
+            whole_wait(pw_v.at[slot, :, :, other_lanes], wsr.at[slot])
         whole_wait(gb_v.at[g], gr.at[g])
-        blocks = []
         for i in range(2):
             got = gb_v[g, :, i].astype(F32)
-            blocks.append(jnp.concatenate([got[:, :8].reshape(128, 128), got[:, 8:].reshape(128, 128)], 1))
-        rows = jnp.concatenate(blocks, 0).astype(BF16)
-        for i, a in enumerate(group_slots(g)):
-            cc_v[a] = rows[i * 64 : (i + 1) * 64]
+            rows = jnp.concatenate([got[:, :8].reshape(128, 128), got[:, 8:].reshape(128, 128)], 1).astype(BF16)
+            cc_v[slots[i]] = rows[:64]
+            cc_v[slots[2 + i]] = rows[64:]
 
         def one(m):
-            terms = dot(rows, p2_v[m])
-            for i, a in enumerate(group_slots(g)):
-                pr_v[a, m] = terms[i * 64 : (i + 1) * 64]
-
-        for m in range(3):
-            one(m)
+            terms = acc_v[m]
+            for slot in slots:
+                terms = terms + dot(cc_v[slot], pw_v[slot, m])
+            acc_v[m] = terms
+
+        loop(0, 3, one)
 
     def turn_of(i):
         more = i < GROUPS - 1
@@ -311,15 +354,14 @@
             whole_wait(wt_v.at[core], wr.at[0])
             remote(wt_v.at[core], wt_v.at[core], ws.at[2], wr.at[3], sibling)
             pw_own.wait()
-            whole_wait(pw_v.at[1 - core], wr.at[1])
-            for m in range(3):
-                for part in range(2):
-                    p2_v[m, :, part * 128 : (part + 1) * 128] = pw_v[part, m]
-
-        pl.when(i >= 2)(lambda: project(i - 2))
+            acc_v[...] = jnp.zeros_like(acc_v)
+
         ringing(lambda: odd(parts[2:]))
         pl.when(i == 0)(lambda: turn(core))
-        pl.when((i >= 1) & (i <= GROUPS))(lambda: reduce(i - 1))
+        pl.when((i >= 2) & (i < GROUPS + 2))(lambda: spread(i - 2))
+        pl.when((i >= 1) & (i < GROUPS + 1))(lambda: reduce(i - 1))
+        pl.when(i == GROUPS)(lambda: weights_step(7, False))
+        pl.when(i == GROUPS + 1)(weights_end)
         ringing(lambda: even(parts))
 
         @pl.when(i == 0)
@@ -327,88 +369,11 @@
             whole_wait(wt_v.at[1 - core], wr.at[3])
             turn(1 - core)
 
+        ringing(lambda: weights_step(i + 3))
         ringing(lambda: conv(i))
-
-    loop(0, GROUPS + 2, turn_of)
-
-    def place_of(offset):
-        return jnp.where(offset <= 0, -offset, 7 + offset)
-
-    def add_right(k, m):
-        whole_wait(rr_v.at[k - 1, m], rs_r.at[0, k - 1, m])
-        term = rr_v[k - 1, m].astype(F32) + pr_v[place_of(TO_RIGHT[m] - SHIFT[m] - k), m]
-        sr_v[k, m] = term.astype(BF16)
-        remote(sr_v.at[k, m], rr_v.at[k, m], rs_s.at[0, k, m], rs_r.at[0, k, m], right)
-
-    def add_left(k, m):
-        whole_wait(rl_v.at[k - 1, m], rs_r.at[1, k - 1, m])
-        term = rl_v[k - 1, m].astype(F32) + pr_v[place_of(k - (15 - TO_RIGHT[m]) - SHIFT[m]), m]
-        sl_v[k, m] = term.astype(BF16)
-        remote(sl_v.at[k, m], rl_v.at[k, m], rs_s.at[1, k, m], rs_r.at[1, k, m], left)
-
-    for m in ORDER:
-        sr_v[0, m] = pr_v[slot_of(7), m].astype(BF16)
-        remote(sr_v.at[0, m], rr_v.at[0, m], rs_s.at[0, 0, m], rs_r.at[0, 0, m], right)
-        sl_v[0, m] = pr_v[slot_of(8), m].astype(BF16)
-        remote(sl_v.at[0, m], rl_v.at[0, m], rs_s.at[1, 0, m], rs_r.at[1, 0, m], left)
-
-    offset = lax.rem(zt - z + NZ, NZ)
-    place = jnp.where(offset == 0, 0, jnp.where(offset <= 8, 7 + offset, NZ - offset))
-
-    @pl.when(zt != z)
-    def _():
-        remote(cc_v.at[place], r1_v, r1s.at[0], r1r.at[0], far)
-
-    @pl.when(zt == z)
-    def _():
-        pltpu.make_async_copy(cc_v.at[place], r1_v, r1r.at[0]).start()
-
-    for i in range(4):
-        whole_wait(pk_v.at[0], fs.at[i])
-    whole_wait(wt_v.at[0, pl.ds(0, 7)], ws.at[0])
-    pw_cp.wait_send()
-    whole_wait(wt_v.at[0], ws.at[2])
-    for hp in range(2):
-        whole_wait(ts_v.at[hp, pl.ds(0, 7)], as_.at[hp])
-
-    @pl.when(core != half)
-    def _():
-        for hp in range(2):
-            whole_wait(ts_v.at[hp, 0], as_.at[2 + hp])
-
-    def ring_left(k):
-        for c in range(2):
-            for way in range(2):
-                whole_wait(acts.at[0, 0, c], zs.at[way, k, way, c])
-                pl.when(k < 7)(lambda: whole_wait(acts.at[0, 0, c], zs.at[way, k, 1 - way, c]))
-
-    loop(0, 8, ring_left)
-    loop(0, GROUPS, lambda g: whole_wait(sb_v.at[g, pl.ds(0, 15)], ss.at[g]))
-
-    def sums(k):
-        for m in ORDER:
-            add_right(k, m)
-            add_left(k, m)
-
-        @pl.when(k == 4)
-        def _():
-            whole_wait(r1_v, r1r.at[0])
-
-            @pl.when(z != 0)
-            def _():
-                remote(r1_v, res_v, r1s.at[1], r1r.at[1], chip_at(zt))
-
-            @pl.when(z == 0)
-            def _():
-                pltpu.make_async_copy(r1_v, res_v, r1r.at[1]).start()
-
-    loop(1, 7, sums)
-    loop(0, GROUPS, lambda g: whole_wait(sb_v.at[g, pl.ds(0, 15)], gs.at[g]))
-    for m in ORDER:
-        if TO_RIGHT[m] == 8:
-            add_right(7, m)
-        else:
-            add_left(7, m)
+        pl.when(i >= 3)(lambda: project(i - 3))
+
+    loop(0, GROUPS + 3, turn_of)
 
     first = core == 0
 
@@ -417,56 +382,73 @@
         xs_v[i] = jnp.where(first, both[:, 128:], both[:, :128])
         return remote(xs_v.at[i], f_v.at[i, core], xs.at[i], xr.at[i], sibling)
 
-    whole_wait(res_v, r1r.at[1])
-    swaps = [exchange(1, res_v[...])]
+    offset = lax.rem(chip - z + NZ, NZ)
+    place = jnp.where(offset == 0, 0, jnp.where(offset <= 8, 7 + offset, NZ - offset))
+    swaps = [exchange(1, cc_v[place])]
     kv_cp = []
     for m in ORDER:
-        nr = TO_RIGHT[m]
-        whole_wait(rr_v.at[nr - 1, m], rs_r.at[0, nr - 1, m])
-        whole_wait(rl_v.at[14 - nr, m], rs_r.at[1, 14 - nr, m])
-        both = pr_v[slot_of(-SHIFT[m]), m] + rr_v[nr - 1, m].astype(F32) + rl_v[14 - nr, m].astype(F32)
-        both = both.astype(BF16)
+        both = acc_v[m].astype(BF16)
         if m == 0:
             swaps.append(exchange(0, both))
             continue
         i = m - 1
         for c in range(2):
             ys_v[i, c] = both[:, c * 128 : (c + 1) * 128]
-        kv_v[i, 1, core] = jnp.where(first, both[:, :128], both[:, 128:])
-        for back, away in ((3, 2), (2, 1), (0, NZ - 1)):
+        kv_v[i, 0, core] = jnp.where(first, both[:, :128], both[:, 128:])
+        for back in (3, 2, 1):
             for c in range(2):
                 kv_cp.append(
                     remote(
-                        ys_v.at[i, c], kv_v.at[i, back, core], ks.at[i, back, c], kr.at[i, back, core], plane_at(away, c)
+                        ys_v.at[i, c], kv_v.at[i, back, core], ks.at[i, back, c], kr.at[i, back, core], plane_at(back, c)
                     )
                 )
         kv_cp.append(
-            remote(ys_v.at[i, 1 - core], kv_v.at[i, 1, core], ks.at[i, 1, 0], kr.at[i, 1, core], sibling)
+            remote(ys_v.at[i, 1 - core], kv_v.at[i, 0, core], ks.at[i, 0, 0], kr.at[i, 0, core], sibling)
         )
-    def sums_left(k):
-        for m in ORDER:
+    for i in range(4):
+        whole_wait(pk_v.at[0], fs.at[i])
+    whole_wait(wt_v.at[0, pl.ds(0, 7)], ws.at[0])
+    whole_wait(wt_v.at[0], ws.at[2])
+    for hp in range(2):
+        whole_wait(ts_v.at[hp, pl.ds(0, 7)], as_.at[hp])
+
+    @pl.when(core != half)
+    def _():
+        for hp in range(2):
+            whole_wait(ts_v.at[hp, 0], as_.at[2 + hp])
+
+    def ring_left(k):
+        for c in range(2):
             for way in range(2):
-                whole_wait(sr_v.at[0, m], rs_s.at[way, k, m])
-
-    loop(0, 7, sums_left)
-    for m in ORDER:
-        whole_wait(sr_v.at[0, m], rs_s.at[0 if TO_RIGHT[m] == 8 else 1, 7, m])
-
-    @pl.when(zt != z)
-    def _():
-        whole_wait(r1_v, r1s.at[0])
-
-    @pl.when(z != 0)
-    def _():
-        whole_wait(r1_v, r1s.at[1])
-
+                whole_wait(acts.at[0, 0, c], zs.at[way, k, way, c])
+                pl.when(k < 7)(lambda: whole_wait(acts.at[0, 0, c], zs.at[way, k, 1 - way, c]))
+
+    loop(0, 8, ring_left)
+    loop(0, GROUPS, lambda g: whole_wait(sb_v.at[g, pl.ds(0, 15)], ss.at[g]))
+
+    loop(0, GROUPS, lambda g: whole_wait(sb_v.at[g, pl.ds(0, 15)], gs.at[g]))
+
+    def chunks_left(g):
+        for i in range(2):
+            pl.when((g + i > 0) | (chip >= 8))(lambda: whole_wait(gt_v.at[0, 0], hs.at[g, i]))
+
+    loop(0, GROUPS, chunks_left)
+
+    def weights_left(k):
+        for way in range(2):
+            whole_wait(held(0), wzs.at[way, k])
+
+    loop(0, 7, weights_left)
+    whole_wait(pw_v.at[15, 2, :, lanes], wzs.at[0, 7])
+    whole_wait(pw_v.at[15, pl.ds(0, 2), :, lanes], wzs.at[1, 7])
+    loop(0, NZ, lambda k: whole_wait(held(0), wss.at[k]))
     for i in range(2):
         whole_wait(f_v.at[i, 1 - core], xr.at[i])
     for cp in swaps:
         cp.wait_send()
     for i in range(2):
-        whole_wait(kv_v.at[i, 1, 1 - core], kr.at[i, 1, 1 - core])
-        for back in (0, 2, 3):
+        whole_wait(kv_v.at[i, 0, 1 - core], kr.at[i, 0, 1 - core])
+        for back in (1, 2, 3):
             for c in range(2):
                 whole_wait(kv_v.at[i, back, c], kr.at[i, back, c])
 
@@ -512,20 +494,14 @@
         vmem((16, 2, 2, 4, 16, 256), BF16),
         vmem((2, 8, 32, 512), BF16),
         vmem((2, 512, 256), BF16),
-        vmem((2, 3, 256, 128), BF16),
-        vmem((3, 256, 256), BF16),
+        vmem((16, 3, 256, 256), BF16),
         vmem((4, 16, 2, 16, 128), BF16),
         vmem((4, 16, 2, 16, 128), BF16),
         vmem((4, 2, 16, 128), BF16),
+        vmem((4, 2, 16, 128), BF16),
         vmem((4, 16, 2, 16, 128), BF16),
         vmem((16, 64, 256), BF16),
-        vmem((16, 3, 64, 256), F32),
-        vmem((8, 3, 64, 256), BF16),
-        vmem((8, 3, 64, 256), BF16),
-        vmem((8, 3, 64, 256), BF16),
-        vmem((8, 3, 64, 256), BF16),
-        vmem((64, 256), BF16),
-        vmem((64, 256), BF16),
+        vmem((3, 64, 256), F32),
         vmem((2, 64, 128), BF16),
         vmem((2, 2, 64, 128), BF16),
         vmem((2, 2, 64, 128), BF16),
@@ -534,8 +510,8 @@
         dma((4,)), dma((4,)), dma((4,)), dma((3,)), dma((4,)), dma((4,)), dma((2,)),
         dma((2, 8, 2, 2)), dma((2, 8, 2, 2)),
         dma((4,)), dma((4,)), dma((4,)), dma((4,)),
-        dma((2, 8, 3)), dma((2, 8, 3)),
-        dma((2,)), dma((2,)), dma((2,)), dma((2,)),
+        dma((4, 2)), dma((4, 2)), dma((2, 8)), dma((2, 8)), dma((16,)), dma((16,)),
+        dma((2,)), dma((2,)),
         dma((2, 4, 2)), dma((2, 4, 2)), dma((2,)),
     ]
     return pl.pallas_call(

time: 114 us -> 108 us (0.947)
  Pallas kernels: 111 us -> 105 us
    pallas_call x1, Pallas kernels: 111 us -> 105 us  [per_device(): pl.pallas_call(kernel, out_shape=(jax.ShapeDtypeStruct((128, 512), BF16),...]
where the time goes in v4:
time: 108 us
  Pallas kernels  105 us (97%)
  local copies, waits for them, and re-layouts  2.19 us (2%)
    pallas_call x1, Pallas kernels, per_device(): pl.pallas_call(kernel, out_shape=(jax.ShapeDtypeStruct((128, 512), BF16),...  105 us
    unnamed x4, local copies, waits for them, and re-layouts  2.19 us

profile of v4, /device:TPU:1, one launch (start us, length us, event | category | flops | bytes accessed | tf_op | source)
XLA Modules:
  0.0 108.0 jit_solution(15374387744601269852)
XLA Ops:
  0.6 105.1 %shard_map.77 = (bf16[128,512]{1,0:T(8,128)(2,1)}, bf16[1,128,128]{2,1,0:T(8,128)(2,1)}) custom-call(bf16[128,512]{1,0:T(8,128)(2,1)} %q_in.1, bf16[128,512]{1,0:T(8,128)(2,1)} %k_in.1, bf16[128,512]{1,0:T(8,128)(2,1)} %v_in.1, bf16[128,512]{1,0:T(8,128)(2,1)} %x_in.1, bf16[8,32,512]{2,1,0:T(8,128)(2,1)} %bitcast.4, bf16[3,256,128]{2,1,0:T(8,128)(2,1)} %bitcast.5), custom_call_target="tpu_custom_call" | custom-call | tf_op jit(solution)/shard_map/pallas_call | solution.py:517
  105.8 0.0 copy-start
  105.8 1.6 %copy.10 = bf16[128,512]{1,0:T(8,128)(2,1)} copy(bf16[128,512]{1,0:T(8,128)(2,1)} %get-tuple-element.4) | data formatting | bytes 262144
  107.4 0.0 copy-done
  107.4 0.6 copy.11
Async XLA Ops:
  105.8 1.6 %copy-start = (bf16[1,128,128]{2,1,0:T(8,128)(2,1)S(1)}, bf16[1,128,128]{2,1,0:T(8,128)(2,1)}, u32[]{:S(2)}) copy-start(bf16[1,128,128]{2,1,0:T(8,128)(2,1)} %get-tuple-element.5) | copy-start | bytes 98308

commit v5 on v4

--- a/solution.py
+++ b/solution.py
@@ -91,12 +91,12 @@
     for dev in (after, before):
         greet(dev)
     loop(1, NZ, lambda j: greet(plane_at(j, core)))
-    for away in (1, 2, 3, NZ - 3, NZ - 2, NZ - 1):
+    for away in (1, 2, NZ - 2, NZ - 1):
         greet(plane_at(away, 1 - core))
     loop(1, 16, lambda j: greet(chip_at(lax.rem(chip + j, 16))))
     loop(0, 8, lambda j: greet((z * 8 + j, 2 * yl + 1 - core)))
 
-    pl.semaphore_wait(barrier, 46)
+    pl.semaphore_wait(barrier, 44)
 
     fine_cp = []
     for hp in range(2):
@@ -107,34 +107,44 @@
     lanes = pl.ds(pl.multiple_of(core * 128, 128), 128)
     other_lanes = pl.ds(pl.multiple_of((1 - core) * 128, 128), 128)
 
-    def held(slot):
-        return pw_v.at[slot, :, :, lanes]
-
-    pw_own = pltpu.make_async_copy(pw_in, held(0), wr.at[2])
+    def held(slot, m):
+        return pw_v.at[slot, m, :, lanes]
+
+    pw_own = pltpu.make_async_copy(pw_in, pw_v.at[0, :, :, lanes], wr.at[2])
     pw_own.start()
-    remote(pw_in, held(1), wzs.at[0, 0], wzr.at[0, 0], right)
-    remote(pw_in, held(8), wzs.at[1, 0], wzr.at[1, 0], left)
-    remote(pw_in, held(0), wss.at[0], wsr.at[0], sibling)
-
-    def weights_step(k, on=True):
-        whole_wait(held(k), wzr.at[0, k - 1])
-        if on:
-            remote(held(k), held(k + 1), wzs.at[0, k], wzr.at[0, k], right)
-        else:
-            remote(pw_v.at[7, 2, :, lanes], pw_v.at[15, 2, :, lanes], wzs.at[0, 7], wzr.at[0, 7], right)
-        whole_wait(held(7 + k), wzr.at[1, k - 1])
-        if on:
-            remote(held(7 + k), held(8 + k), wzs.at[1, k], wzr.at[1, k], left)
-        else:
-            two = pl.ds(0, 2)
-            remote(pw_v.at[14, two, :, lanes], pw_v.at[15, two, :, lanes], wzs.at[1, 7], wzr.at[1, 7], left)
-        remote(held(k), held(k), wss.at[k], wsr.at[k], sibling)
-        remote(held(7 + k), held(7 + k), wss.at[7 + k], wsr.at[7 + k], sibling)
+    for m in range(3):
+        remote(pw_in.at[m], held(1, m), wzs.at[0, 0, m], wzr.at[0, 0, m], right)
+        remote(pw_in.at[m], held(8, m), wzs.at[1, 0, m], wzr.at[1, 0, m], left)
+    for m in range(3):
+        remote(pw_in.at[m], held(0, m), wss.at[0, m], wsr.at[0, m], sibling)
+
+    def weights_step(k, m):
+        whole_wait(held(k, m), wzr.at[0, k - 1, m])
+        whole_wait(held(7 + k, m), wzr.at[1, k - 1, m])
+
+        @pl.when((k < 7) | (m == 2))
+        def _():
+            remote(held(k, m), held(jnp.where(k == 7, 15, k + 1), m), wzs.at[0, k, m], wzr.at[0, k, m], right)
+
+        @pl.when((k < 7) | (m != 2))
+        def _():
+            remote(held(7 + k, m), held(8 + k, m), wzs.at[1, k, m], wzr.at[1, k, m], left)
+
+        @pl.when((k == 7) & (m == 2))
+        def _():
+            remote(held(7, m), held(15, m), wss.at[15, m], wsr.at[15, m], plane_at(1, 1 - core))
+
+        @pl.when((k == 7) & (m != 2))
+        def _():
+            remote(held(14, m), held(15, m), wss.at[15, m], wsr.at[15, m], plane_at(NZ - 1, 1 - core))
+
+        remote(held(k, m), held(k, m), wss.at[k, m], wsr.at[k, m], sibling)
+        remote(held(7 + k, m), held(7 + k, m), wss.at[7 + k, m], wsr.at[7 + k, m], sibling)
 
     def weights_end():
-        whole_wait(pw_v.at[15, 2, :, lanes], wzr.at[0, 7])
-        whole_wait(pw_v.at[15, pl.ds(0, 2), :, lanes], wzr.at[1, 7])
-        remote(held(15), held(15), wss.at[15], wsr.at[15], sibling)
+        for m in range(3):
+            way = 0 if m == 2 else 1
+            whole_wait(held(15, m), wzr.at[way, 7, m])
 
     row = lax.broadcasted_iota(jnp.int32, (128, 128), 0)
     col = lax.broadcasted_iota(jnp.int32, (128, 128), 1)
@@ -192,7 +202,10 @@
         def _():
             remote(ts_v.at[hp, s], acts.at[0, hp, core, quarter], as_.at[2 + hp], ar.at[hp], sibling)
 
-        pl.when(hp == 0)(lambda: weights_step(1))
+        @pl.when(hp == 0)
+        def _():
+            loop(0, 2, lambda m: weights_step(1, m))
+
 
     loop(0, 2, whole_part)
 
@@ -234,7 +247,8 @@
 
     loop(1, 8, send_weights)
     pltpu.make_async_copy(cw_in.at[s], wt_v.at[core, s], wr.at[0]).start()
-    weights_step(2)
+    weights_step(1, 2)
+    loop(0, 3, lambda m: weights_step(2, m))
     fo_cp = pltpu.make_async_copy(fo_v, fine_out, out_sem.at[0])
     fo_cp.start()
 
@@ -272,7 +286,7 @@
 
         for i in range(2):
             p = 2 * g + i
-            away = jnp.where(chip < 8, lax.rem(NZ - p, NZ), p + 1)
+            away = jnp.where(chip < 8, lax.rem(NZ + 1 - p, NZ), p + 2)
 
             @pl.when(away != 0)
             def _():
@@ -293,12 +307,16 @@
         pltpu.make_async_copy(gt_v.at[g], gb_v.at[g, chip], gr.at[g]).start()
 
     def weight_slots(g):
-        return [jnp.where(g == 0, 0, 7 + 2 * g), 8 + 2 * g, 2 * g + 1, jnp.where(g == 3, 15, 2 * g + 2)]
+        return [
+            jnp.where(g == 0, 1, 6 + 2 * g), jnp.where(g == 0, 0, 7 + 2 * g),
+            jnp.where(g == 3, 15, 2 * g + 2), jnp.where(g == 3, 14, 2 * g + 3),
+        ]
 
     def project(g):
         slots = weight_slots(g)
         for slot in slots:
-            whole_wait(pw_v.at[slot, :, :, other_lanes], wsr.at[slot])
+            for m in range(3):
+                whole_wait(pw_v.at[slot, m, :, other_lanes], wsr.at[slot, m])
         whole_wait(gb_v.at[g], gr.at[g])
         for i in range(2):
             got = gb_v[g, :, i].astype(F32)
@@ -357,53 +375,65 @@
             acc_v[...] = jnp.zeros_like(acc_v)
 
         ringing(lambda: odd(parts[2:]))
+        weighing = pl.when(i < GROUPS - 1)
+        weighing(lambda: weights_step(i + 3, 0))
         pl.when(i == 0)(lambda: turn(core))
         pl.when((i >= 2) & (i < GROUPS + 2))(lambda: spread(i - 2))
         pl.when((i >= 1) & (i < GROUPS + 1))(lambda: reduce(i - 1))
-        pl.when(i == GROUPS)(lambda: weights_step(7, False))
-        pl.when(i == GROUPS + 1)(weights_end)
-        ringing(lambda: even(parts))
+        pl.when(i == GROUPS + 2)(weights_end)
+        ringing(lambda: even(parts[:2]))
+        weighing(lambda: weights_step(i + 3, 1))
+        ringing(lambda: even(parts[2:]))
+        weighing(lambda: weights_step(i + 3, 2))
 
         @pl.when(i == 0)
         def _():
             whole_wait(wt_v.at[1 - core], wr.at[3])
             turn(1 - core)
 
-        ringing(lambda: weights_step(i + 3))
         ringing(lambda: conv(i))
+
+        @pl.when((i == GROUPS - 1) | (i == GROUPS))
+        def _():
+            loop(0, 3, lambda m: weights_step(i + 3, m))
+
         pl.when(i >= 3)(lambda: project(i - 3))
 
     loop(0, GROUPS + 3, turn_of)
 
     first = core == 0
 
-    def exchange(i, both):
-        f_v[i, core] = jnp.where(first, both[:, :128], both[:, 128:])
-        xs_v[i] = jnp.where(first, both[:, 128:], both[:, :128])
-        return remote(xs_v.at[i], f_v.at[i, core], xs.at[i], xr.at[i], sibling)
+    swaps = []
+
+    def send_back(i, both):
+        for c in range(2):
+            xs_v[i, c] = both[:, c * 128 : (c + 1) * 128]
+            swaps.append(
+                remote(xs_v.at[i, c], f_v.at[i, core], xs.at[i, c], xr.at[i, core], plane_at(NZ - 1, c))
+            )
 
     offset = lax.rem(chip - z + NZ, NZ)
     place = jnp.where(offset == 0, 0, jnp.where(offset <= 8, 7 + offset, NZ - offset))
-    swaps = [exchange(1, cc_v[place])]
+    send_back(1, cc_v[place])
     kv_cp = []
     for m in ORDER:
         both = acc_v[m].astype(BF16)
         if m == 0:
-            swaps.append(exchange(0, both))
+            send_back(0, both)
             continue
         i = m - 1
         for c in range(2):
             ys_v[i, c] = both[:, c * 128 : (c + 1) * 128]
-        kv_v[i, 0, core] = jnp.where(first, both[:, :128], both[:, 128:])
-        for back in (3, 2, 1):
+        kv_v[i, 1, core] = jnp.where(first, both[:, :128], both[:, 128:])
+        for back, away in ((3, 2), (2, 1), (0, NZ - 1)):
             for c in range(2):
                 kv_cp.append(
                     remote(
-                        ys_v.at[i, c], kv_v.at[i, back, core], ks.at[i, back, c], kr.at[i, back, core], plane_at(back, c)
+                        ys_v.at[i, c], kv_v.at[i, back, core], ks.at[i, back, c], kr.at[i, back, core], plane_at(away, c)
                     )
                 )
         kv_cp.append(
-            remote(ys_v.at[i, 1 - core], kv_v.at[i, 0, core], ks.at[i, 0, 0], kr.at[i, 0, core], sibling)
+            remote(ys_v.at[i, 1 - core], kv_v.at[i, 1, core], ks.at[i, 1, 0], kr.at[i, 1, core], sibling)
         )
     for i in range(4):
         whole_wait(pk_v.at[0], fs.at[i])
@@ -430,25 +460,27 @@
 
     def chunks_left(g):
         for i in range(2):
-            pl.when((g + i > 0) | (chip >= 8))(lambda: whole_wait(gt_v.at[0, 0], hs.at[g, i]))
+            pl.when((2 * g + i != 1) | (chip >= 8))(lambda: whole_wait(gt_v.at[0, 0], hs.at[g, i]))
 
     loop(0, GROUPS, chunks_left)
 
     def weights_left(k):
         for way in range(2):
-            whole_wait(held(0), wzs.at[way, k])
+            for m in range(3):
+                whole_wait(held(0, m), wzs.at[way, k, m])
 
     loop(0, 7, weights_left)
-    whole_wait(pw_v.at[15, 2, :, lanes], wzs.at[0, 7])
-    whole_wait(pw_v.at[15, pl.ds(0, 2), :, lanes], wzs.at[1, 7])
-    loop(0, NZ, lambda k: whole_wait(held(0), wss.at[k]))
+    for m in range(3):
+        whole_wait(held(0, m), wzs.at[0 if m == 2 else 1, 7, m])
+    loop(0, NZ, lambda k: [whole_wait(held(0, m), wss.at[k, m]) for m in range(3)])
     for i in range(2):
-        whole_wait(f_v.at[i, 1 - core], xr.at[i])
+        for c in range(2):
+            whole_wait(f_v.at[i, c], xr.at[i, c])
     for cp in swaps:
         cp.wait_send()
     for i in range(2):
-        whole_wait(kv_v.at[i, 0, 1 - core], kr.at[i, 0, 1 - core])
-        for back in (1, 2, 3):
+        whole_wait(kv_v.at[i, 1, 1 - core], kr.at[i, 1, 1 - core])
+        for back in (0, 2, 3):
             for c in range(2):
                 whole_wait(kv_v.at[i, back, c], kr.at[i, back, c])
 
@@ -502,7 +534,7 @@
         vmem((4, 16, 2, 16, 128), BF16),
         vmem((16, 64, 256), BF16),
         vmem((3, 64, 256), F32),
-        vmem((2, 64, 128), BF16),
+        vmem((2, 2, 64, 128), BF16),
         vmem((2, 2, 64, 128), BF16),
         vmem((2, 2, 64, 128), BF16),
         vmem((2, 4, 2, 64, 128), BF16),
@@ -510,8 +542,8 @@
         dma((4,)), dma((4,)), dma((4,)), dma((3,)), dma((4,)), dma((4,)), dma((2,)),
         dma((2, 8, 2, 2)), dma((2, 8, 2, 2)),
         dma((4,)), dma((4,)), dma((4,)), dma((4,)),
-        dma((4, 2)), dma((4, 2)), dma((2, 8)), dma((2, 8)), dma((16,)), dma((16,)),
-        dma((2,)), dma((2,)),
+        dma((4, 2)), dma((4, 2)), dma((2, 8, 3)), dma((2, 8, 3)), dma((16, 3)), dma((16, 3)),
+        dma((2, 2)), dma((2, 2)),
         dma((2, 4, 2)), dma((2, 4, 2)), dma((2,)),
     ]
     return pl.pallas_call(

time: 108 us -> 107 us (level)
  no operation moved by 1% of the time
where the time goes in v5:
time: 107 us
  Pallas kernels  104 us (97%)
  local copies, waits for them, and re-layouts  2.19 us (2%)
    pallas_call x1, Pallas kernels, per_device(): pl.pallas_call(kernel, out_shape=(jax.ShapeDtypeStruct((128, 512), BF16),...  104 us
    unnamed x4, local copies, waits for them, and re-layouts  2.19 us

profile of v5, /device:TPU:1, one launch (start us, length us, event | category | flops | bytes accessed | tf_op | source)
XLA Modules:
  0.0 107.3 jit_solution(12941109290026477122)
XLA Ops:
  0.6 104.4 %shard_map.77 = (bf16[128,512]{1,0:T(8,128)(2,1)}, bf16[1,128,128]{2,1,0:T(8,128)(2,1)}) custom-call(bf16[128,512]{1,0:T(8,128)(2,1)} %q_in.1, bf16[128,512]{1,0:T(8,128)(2,1)} %k_in.1, bf16[128,512]{1,0:T(8,128)(2,1)} %v_in.1, bf16[128,512]{1,0:T(8,128)(2,1)} %x_in.1, bf16[8,32,512]{2,1,0:T(8,128)(2,1)} %bitcast.4, bf16[3,256,128]{2,1,0:T(8,128)(2,1)} %bitcast.5), custom_call_target="tpu_custom_call" | custom-call | tf_op jit(solution)/shard_map/pallas_call | solution.py:549
  105.1 0.0 copy-start
  105.1 1.6 %copy.10 = bf16[128,512]{1,0:T(8,128)(2,1)} copy(bf16[128,512]{1,0:T(8,128)(2,1)} %get-tuple-element.4) | data formatting | bytes 262144
  106.7 0.0 copy-done
  106.7 0.6 copy.11
Async XLA Ops:
  105.1 1.6 %copy-start = (bf16[1,128,128]{2,1,0:T(8,128)(2,1)S(1)}, bf16[1,128,128]{2,1,0:T(8,128)(2,1)}, u32[]{:S(2)}) copy-start(bf16[1,128,128]{2,1,0:T(8,128)(2,1)} %get-tuple-element.5) | copy-start | bytes 98308

commit v6 on v3

--- a/solution.py
+++ b/solution.py
@@ -14,15 +14,15 @@
 SCALE = HEAD_DIM ** -0.5
 NEG = -1e30
 GROUPS = 4
-TO_RIGHT = (7, 8, 8)
+TO_RIGHT = (3, 4, 4)
 SHIFT = (0, 1, 1)
 ORDER = (1, 2, 0)
 
 
 def slot_of(offset):
-    if offset == -8:
-        offset = 8
-    return -offset if offset <= 0 else 7 + offset
+    if offset == -4:
+        offset = 4
+    return -offset if offset <= 0 else 3 + offset
 
 
 def dot_t(a, b):
@@ -41,7 +41,7 @@
     q_in, k_in, v_in, x_in, cw_in, pw_in, fine_out, coarse_out,
     q_v, k_v, v_v, x_v, pk_v, pv_v, mix_v, st_v, fo_v, ts_v, acts, wt_v, w2_v, pw_v, p2_v,
     sb_v, rb_v, gs_v, gb_v, cc_v, pr_v, rr_v, rl_v, sr_v, sl_v, r1_v, res_v, xs_v, f_v, ys_v, kv_v, co_v,
-    in_sem, fs, fr, ws, wr, as_, ar, zs, zr, ss, sr, gs, gr, rs_s, rs_r, r1s, r1r, xs, xr, ks, kr, out_sem,
+    in_sem, fs, fr, ws, wr, as_, ar, zs, zr, ss, sr, gs, gr, pws, pwr, rs_s, rs_r, r1s, r1r, xs, xr, ks, kr, out_sem,
 ):
     ctx = lax.axis_index("ctx")
     head = lax.axis_index("head")
@@ -55,10 +55,14 @@
     sibling = (ctx, 2 * yl + 1 - core)
     after = (lax.rem(ctx + 1, 128), head)
     before = (lax.rem(ctx + 127, 128), head)
-    right = (lax.rem(z + 1, NZ) * 8 + s, head)
-    left = (lax.rem(z + NZ - 1, NZ) * 8 + s, head)
-    zt = lax.rem(chip - z + NZ, NZ)
-    far = (zt * 8 + s, head)
+    right = (lax.rem(z + 2, NZ) * 8 + s, head)
+    left = (lax.rem(z + NZ - 2, NZ) * 8 + s, head)
+    side = lax.rem(z, 2)
+    place_z = lax.div(z, 2)
+    twin = z + 1 - 2 * side
+    ahead = lax.rem(lax.div(chip, 2) - place_z + 8, 8)
+    far = ((2 * ahead + side) * 8 + s, head)
+    to_chip = 2 * ahead + lax.rem(chip, 2)
 
     def chip_at(c):
         return (z * 8 + lax.div(c, 2), lax.rem(c, 2) * 2 + core)
@@ -100,12 +104,13 @@
 
     loop(1, 16, lambda j: greet(chip_at(lax.rem(chip + j, 16))))
     loop(0, 8, lambda j: greet((z * 8 + j, 2 * yl + 1 - core)))
-
-    @pl.when(zt != z)
+    loop(0, 8, lambda j: greet((twin * 8 + j, head)))
+
+    @pl.when(ahead != place_z)
     def _():
         greet(far)
 
-    pl.semaphore_wait(barrier, 33 + jnp.where(zt != z, 1, 0))
+    pl.semaphore_wait(barrier, 41 + jnp.where(ahead != place_z, 1, 0))
 
     fine_cp = []
     for hp in range(2):
@@ -133,9 +138,25 @@
     loop(0, 2, own_part)
     has_before = ctx > 0
 
+    def send_weights(j):
+        to = lax.rem(s + j, 8)
+        remote(cw_in.at[to], wt_v.at[side, core, s], ws.at[3], wr.at[4], (twin * 8 + to, head))
+
+        @pl.when(j > 0)
+        def _():
+            remote(cw_in.at[to], wt_v.at[side, core, s], ws.at[0], wr.at[0], (z * 8 + to, head))
+
+    def all_weights():
+        loop(0, 8, send_weights)
+        pltpu.make_async_copy(cw_in.at[s], wt_v.at[side, core, s], wr.at[0]).start()
+        for i, (at_z, c) in enumerate([(z, 1 - core), (twin, core), (twin, 1 - core)]):
+            remote(pw_in, pw_v.at[side, core], pws.at[i], pwr.at[side, core], (at_z * 8 + s, 2 * yl + c))
+        pltpu.make_async_copy(pw_in, pw_v.at[side, core], pwr.at[side, core]).start()
+
     def whole_part(hp):
         whole_wait(pk_v.at[hp], fr.at[2 * hp])
         whole_wait(pv_v.at[hp], fr.at[2 * hp + 1])
+        pl.when(hp == 1)(all_weights)
         for j in range(2):
             i = 2 * hp + j
             cols = pl.ds(pl.multiple_of(i * 128, 128), 128)
@@ -174,10 +195,10 @@
     parts = [(hp, c) for hp in range(2) for c in range(2)]
 
     def place_right(k):
-        return jnp.where(k == 8, 15, k)
+        return jnp.where(k == 4, 7, k)
 
     def place_left(k):
-        return jnp.where(k == 0, 0, 7 + k)
+        return jnp.where(k == 0, 0, 3 + k)
 
     def pass_right(k, hp, c):
         remote(
@@ -203,27 +224,20 @@
             pass_right(1, hp, c)
             pass_left(1, hp, c)
 
-    def send_weights(j):
-        to = lax.rem(s + j, 8)
-        remote(cw_in.at[to], wt_v.at[core, s], ws.at[0], wr.at[0], (z * 8 + to, head))
-
-    loop(1, 8, send_weights)
-    pltpu.make_async_copy(cw_in.at[s], wt_v.at[core, s], wr.at[0]).start()
-    pw_cp = remote(pw_in, pw_v.at[core], ws.at[1], wr.at[1], sibling)
-    pw_own = pltpu.make_async_copy(pw_in, pw_v.at[core], wr.at[2])
-    pw_own.start()
     fo_cp = pltpu.make_async_copy(fo_v, fine_out, out_sem.at[0])
     fo_cp.start()
 
     def turn(c):
-        def part(hp):
-            cols = pl.ds(pl.multiple_of(hp * 256, 256), 256)
-            w2_v[c, cols, :] = wt_v[c, :, :, cols].reshape(256, 256).T
+        def part(p):
+            for hp in range(2):
+                rows = slice(hp * 256, (hp + 1) * 256)
+                cols = pl.ds(pl.multiple_of(p * 256, 256), 256)
+                w2_v[c, rows, cols] = wt_v[p, c, :, :, rows].reshape(256, 256).T
 
         loop(0, 2, part)
 
     def group_slots(g):
-        return [2 * g, 2 * g + 8, 2 * g + 1, 2 * g + 9]
+        return [g, 4 + g]
 
     def conv(g):
         total = None
@@ -232,8 +246,8 @@
             term = dot(rows, w2_v[c, hp * 256 : (hp + 1) * 256, :])
             total = term if total is None else total + term
         for i in range(2):
-            lo = total[i * 128 : (i + 1) * 128, :128].reshape(16, 8, 128)
-            hi = total[i * 128 : (i + 1) * 128, 128:].reshape(16, 8, 128)
+            lo = total[:, i * 256 : i * 256 + 128].reshape(16, 8, 128)
+            hi = total[:, i * 256 + 128 : (i + 1) * 256].reshape(16, 8, 128)
             sb_v[g, :, i] = jnp.concatenate([lo, hi], 1).astype(BF16)
 
         def send(j):
@@ -255,76 +269,59 @@
 
     def project(g):
         whole_wait(gb_v.at[g], gr.at[g])
-        blocks = []
-        for i in range(2):
-            got = gb_v[g, :, i].astype(F32)
-            blocks.append(jnp.concatenate([got[:, :8].reshape(128, 128), got[:, 8:].reshape(128, 128)], 1))
-        rows = jnp.concatenate(blocks, 0).astype(BF16)
-        for i, a in enumerate(group_slots(g)):
-            cc_v[a] = rows[i * 64 : (i + 1) * 64]
-
-        def one(m):
-            terms = dot(rows, p2_v[m])
+        rows = []
+        for p in range(2):
+            got = gb_v[g, :, p].astype(F32)
+            rows.append(
+                jnp.concatenate([got[:, :8].reshape(128, 128), got[:, 8:].reshape(128, 128)], 1).astype(BF16)
+            )
+            for i, a in enumerate(group_slots(g)):
+                cc_v[a, p] = rows[p][i * 64 : (i + 1) * 64]
+        for m in range(3):
+            terms = dot(rows[0], p2_v[0, m]) + dot(rows[1], p2_v[1, m])
             for i, a in enumerate(group_slots(g)):
                 pr_v[a, m] = terms[i * 64 : (i + 1) * 64]
 
-        for m in range(3):
-            one(m)
-
     def turn_of(i):
-        more = i < GROUPS - 1
-
-        def odd(parts):
-            k = 2 * i + 1
+        k = i + 1
+
+        def ring(parts):
             for hp, c in parts:
-                got_right(k, hp, c)
-                got_left(k, hp, c)
-                if hp == 0:
-                    pass_right(k + 1, hp, c)
-                    pl.when(more)(lambda: pass_left(k + 1, hp, c))
-                else:
-                    pass_left(k + 1, hp, c)
-                    pl.when(more)(lambda: pass_right(k + 1, hp, c))
-
-        def even(parts):
-            k = 2 * i + 2
-            for hp, c in parts:
-                if hp == 0:
-                    got_right(k, hp, c)
-                else:
-                    got_left(k, hp, c)
-
-                @pl.when(more)
+                near, farther = (got_right, got_left) if hp == 0 else (got_left, got_right)
+                go, go_too = (pass_right, pass_left) if hp == 0 else (pass_left, pass_right)
+                near(k, hp, c)
+                pl.when(k < 4)(lambda: go(k + 1, hp, c))
+
+                @pl.when(k < 4)
                 def _():
-                    if hp == 0:
-                        got_left(k, hp, c)
-                    else:
-                        got_right(k, hp, c)
-                    pass_right(k + 1, hp, c)
-                    pass_left(k + 1, hp, c)
+                    farther(k, hp, c)
+                    pl.when(k < 3)(lambda: go_too(k + 1, hp, c))
 
         ringing = pl.when(i < GROUPS)
-        ringing(lambda: odd(parts[:2]))
+        ringing(lambda: ring(parts[:2]))
 
         @pl.when(i == 0)
         def _():
-            whole_wait(wt_v.at[core], wr.at[0])
-            remote(wt_v.at[core], wt_v.at[core], ws.at[2], wr.at[3], sibling)
-            pw_own.wait()
-            whole_wait(pw_v.at[1 - core], wr.at[1])
-            for m in range(3):
-                for part in range(2):
-                    p2_v[m, :, part * 128 : (part + 1) * 128] = pw_v[part, m]
+            whole_wait(wt_v.at[side, core], wr.at[0])
+            whole_wait(wt_v.at[1 - side, core], wr.at[4])
+            for p in range(2):
+                remote(wt_v.at[p, core], wt_v.at[p, core], ws.at[1 + p], wr.at[1 + p], sibling)
+            for p in range(2):
+                for c in range(2):
+                    whole_wait(pw_v.at[p, c], pwr.at[p, c])
+                    for m in range(3):
+                        p2_v[p, m, :, c * 128 : (c + 1) * 128] = pw_v[p, c, m]
 
         pl.when(i >= 2)(lambda: project(i - 2))
-        ringing(lambda: odd(parts[2:]))
-        pl.when(i == 0)(lambda: turn(core))
+        ringing(lambda: ring(parts[2:3]))
         pl.when((i >= 1) & (i <= GROUPS))(lambda: reduce(i - 1))
-        ringing(lambda: even(parts))
+        ringing(lambda: ring(parts[3:]))
 
         @pl.when(i == 0)
         def _():
-            whole_wait(wt_v.at[1 - core], wr.at[3])
+            turn(core)
+            for p in range(2):
+                whole_wait(wt_v.at[p, 1 - core], wr.at[1 + p])
             turn(1 - core)
 
         ringing(lambda: conv(i))
@@ -332,7 +329,7 @@
     loop(0, GROUPS + 2, turn_of)
 
     def place_of(offset):
-        return jnp.where(offset <= 0, -offset, 7 + offset)
+        return jnp.where(offset <= 0, -offset, 3 + offset)
 
     def add_right(k, m):
         whole_wait(rr_v.at[k - 1, m], rs_r.at[0, k - 1, m])
@@ -342,32 +339,36 @@
 
     def add_left(k, m):
         whole_wait(rl_v.at[k - 1, m], rs_r.at[1, k - 1, m])
-        term = rl_v[k - 1, m].astype(F32) + pr_v[place_of(k - (15 - TO_RIGHT[m]) - SHIFT[m]), m]
+        term = rl_v[k - 1, m].astype(F32) + pr_v[place_of(k - (7 - TO_RIGHT[m]) - SHIFT[m]), m]
         sl_v[k, m] = term.astype(BF16)
         remote(sl_v.at[k, m], rl_v.at[k, m], rs_s.at[1, k, m], rs_r.at[1, k, m], left)
 
     for m in ORDER:
-        sr_v[0, m] = pr_v[slot_of(7), m].astype(BF16)
+        sr_v[0, m] = pr_v[slot_of(3), m].astype(BF16)
         remote(sr_v.at[0, m], rr_v.at[0, m], rs_s.at[0, 0, m], rs_r.at[0, 0, m], right)
-        sl_v[0, m] = pr_v[slot_of(8), m].astype(BF16)
+        sl_v[0, m] = pr_v[slot_of(4), m].astype(BF16)
         remote(sl_v.at[0, m], rl_v.at[0, m], rs_s.at[1, 0, m], rs_r.at[1, 0, m], left)
 
-    offset = lax.rem(zt - z + NZ, NZ)
-    place = jnp.where(offset == 0, 0, jnp.where(offset <= 8, 7 + offset, NZ - offset))
-
-    @pl.when(zt != z)
+    offset = lax.rem(ahead - place_z + 8, 8)
+    place = jnp.where(offset == 0, 0, jnp.where(offset <= 4, 3 + offset, 8 - offset))
+    columns = cc_v.at[place, lax.rem(chip, 2)]
+
+    @pl.when(ahead != place_z)
     def _():
-        remote(cc_v.at[place], r1_v, r1s.at[0], r1r.at[0], far)
-
-    @pl.when(zt == z)
+        remote(columns, r1_v, r1s.at[0], r1r.at[0], far)
+
+    @pl.when(ahead == place_z)
     def _():
-        pltpu.make_async_copy(cc_v.at[place], r1_v, r1r.at[0]).start()
+        pltpu.make_async_copy(columns, r1_v, r1r.at[0]).start()
 
     for i in range(4):
         whole_wait(pk_v.at[0], fs.at[i])
-    whole_wait(wt_v.at[0, pl.ds(0, 7)], ws.at[0])
-    pw_cp.wait_send()
-    whole_wait(wt_v.at[0], ws.at[2])
+    whole_wait(wt_v.at[0, 0, pl.ds(0, 7)], ws.at[0])
+    whole_wait(wt_v.at[0, 0], ws.at[3])
+    for i in range(2):
+        whole_wait(wt_v.at[0, 0], ws.at[1 + i])
+    for i in range(3):
+        whole_wait(pw_v.at[0, 0], pws.at[i])
     for hp in range(2):
         whole_wait(ts_v.at[hp, pl.ds(0, 7)], as_.at[hp])
 
@@ -380,9 +381,9 @@
         for c in range(2):
             for way in range(2):
                 whole_wait(acts.at[0, 0, c], zs.at[way, k, way, c])
-                pl.when(k < 7)(lambda: whole_wait(acts.at[0, 0, c], zs.at[way, k, 1 - way, c]))
-
-    loop(0, 8, ring_left)
+                pl.when(k < 3)(lambda: whole_wait(acts.at[0, 0, c], zs.at[way, k, 1 - way, c]))
+
+    loop(0, 4, ring_left)
     loop(0, GROUPS, lambda g: whole_wait(sb_v.at[g, pl.ds(0, 15)], ss.at[g]))
 
     def sums(k):
@@ -390,25 +391,25 @@
             add_right(k, m)
             add_left(k, m)
 
-        @pl.when(k == 4)
+        @pl.when(k == 2)
         def _():
             whole_wait(r1_v, r1r.at[0])
 
-            @pl.when(z != 0)
+            @pl.when(place_z != 0)
             def _():
-                remote(r1_v, res_v, r1s.at[1], r1r.at[1], chip_at(zt))
-
-            @pl.when(z == 0)
+                remote(r1_v, res_v, r1s.at[1], r1r.at[1], chip_at(to_chip))
+
+            @pl.when(place_z == 0)
             def _():
                 pltpu.make_async_copy(r1_v, res_v, r1r.at[1]).start()
 
-    loop(1, 7, sums)
+    loop(1, 3, sums)
     loop(0, GROUPS, lambda g: whole_wait(sb_v.at[g, pl.ds(0, 15)], gs.at[g]))
     for m in ORDER:
-        if TO_RIGHT[m] == 8:
-            add_right(7, m)
+        if TO_RIGHT[m] == 4:
+            add_right(3, m)
         else:
-            add_left(7, m)
+            add_left(3, m)
 
     first = core == 0
 
@@ -423,8 +424,8 @@
     for m in ORDER:
         nr = TO_RIGHT[m]
         whole_wait(rr_v.at[nr - 1, m], rs_r.at[0, nr - 1, m])
-        whole_wait(rl_v.at[14 - nr, m], rs_r.at[1, 14 - nr, m])
-        both = pr_v[slot_of(-SHIFT[m]), m] + rr_v[nr - 1, m].astype(F32) + rl_v[14 - nr, m].astype(F32)
+        whole_wait(rl_v.at[6 - nr, m], rs_r.at[1, 6 - nr, m])
+        both = pr_v[slot_of(-SHIFT[m]), m] + rr_v[nr - 1, m].astype(F32) + rl_v[6 - nr, m].astype(F32)
         both = both.astype(BF16)
         if m == 0:
             swaps.append(exchange(0, both))
@@ -432,8 +433,8 @@
         i = m - 1
         for c in range(2):
             ys_v[i, c] = both[:, c * 128 : (c + 1) * 128]
-        kv_v[i, 1, core] = jnp.where(first, both[:, :128], both[:, 128:])
-        for back, away in ((3, 2), (2, 1), (0, NZ - 1)):
+        kv_v[i, 2, core] = jnp.where(first, both[:, :128], both[:, 128:])
+        for back, away in ((0, NZ - 2), (1, NZ - 1), (3, 1)):
             for c in range(2):
                 kv_cp.append(
                     remote(
@@ -441,22 +442,22 @@
                     )
                 )
         kv_cp.append(
-            remote(ys_v.at[i, 1 - core], kv_v.at[i, 1, core], ks.at[i, 1, 0], kr.at[i, 1, core], sibling)
+            remote(ys_v.at[i, 1 - core], kv_v.at[i, 2, core], ks.at[i, 2, 0], kr.at[i, 2, core], sibling)
         )
     def sums_left(k):
         for m in ORDER:
             for way in range(2):
                 whole_wait(sr_v.at[0, m], rs_s.at[way, k, m])
 
-    loop(0, 7, sums_left)
+    loop(0, 3, sums_left)
     for m in ORDER:
-        whole_wait(sr_v.at[0, m], rs_s.at[0 if TO_RIGHT[m] == 8 else 1, 7, m])
-
-    @pl.when(zt != z)
+        whole_wait(sr_v.at[0, m], rs_s.at[0 if TO_RIGHT[m] == 4 else 1, 3, m])
+
+    @pl.when(ahead != place_z)
     def _():
         whole_wait(r1_v, r1s.at[0])
 
-    @pl.when(z != 0)
+    @pl.when(place_z != 0)
     def _():
         whole_wait(r1_v, r1s.at[1])
 
@@ -465,8 +466,8 @@
     for cp in swaps:
         cp.wait_send()
     for i in range(2):
-        whole_wait(kv_v.at[i, 1, 1 - core], kr.at[i, 1, 1 - core])
-        for back in (0, 2, 3):
+        whole_wait(kv_v.at[i, 2, 1 - core], kr.at[i, 2, 1 - core])
+        for back in (0, 1, 3):
             for c in range(2):
                 whole_wait(kv_v.at[i, back, c], kr.at[i, back, c])
 
@@ -509,21 +510,21 @@
         vmem((4, 2, 128, 1), F32),
         vmem((128, 512), BF16),
         vmem((2, 8, 16, 256), BF16),
-        vmem((16, 2, 2, 4, 16, 256), BF16),
-        vmem((2, 8, 32, 512), BF16),
-        vmem((2, 512, 256), BF16),
-        vmem((2, 3, 256, 128), BF16),
-        vmem((3, 256, 256), BF16),
+        vmem((8, 2, 2, 4, 16, 256), BF16),
+        vmem((2, 2, 8, 32, 512), BF16),
+        vmem((2, 512, 512), BF16),
+        vmem((2, 2, 3, 256, 128), BF16),
+        vmem((2, 3, 256, 256), BF16),
         vmem((4, 16, 2, 16, 128), BF16),
         vmem((4, 16, 2, 16, 128), BF16),
         vmem((4, 2, 16, 128), BF16),
         vmem((4, 16, 2, 16, 128), BF16),
-        vmem((16, 64, 256), BF16),
-        vmem((16, 3, 64, 256), F32),
-        vmem((8, 3, 64, 256), BF16),
-        vmem((8, 3, 64, 256), BF16),
-        vmem((8, 3, 64, 256), BF16),
-        vmem((8, 3, 64, 256), BF16),
+        vmem((8, 2, 64, 256), BF16),
+        vmem((8, 3, 64, 256), F32),
+        vmem((4, 3, 64, 256), BF16),
+        vmem((4, 3, 64, 256), BF16),
+        vmem((4, 3, 64, 256), BF16),
+        vmem((4, 3, 64, 256), BF16),
         vmem((64, 256), BF16),
         vmem((64, 256), BF16),
         vmem((2, 64, 128), BF16),
@@ -531,10 +532,10 @@
         vmem((2, 2, 64, 128), BF16),
         vmem((2, 4, 2, 64, 128), BF16),
         vmem((128, 128), BF16),
-        dma((4,)), dma((4,)), dma((4,)), dma((3,)), dma((4,)), dma((4,)), dma((2,)),
-        dma((2, 8, 2, 2)), dma((2, 8, 2, 2)),
+        dma((4,)), dma((4,)), dma((4,)), dma((4,)), dma((5,)), dma((4,)), dma((2,)),
+        dma((2, 4, 2, 2)), dma((2, 4, 2, 2)),
         dma((4,)), dma((4,)), dma((4,)), dma((4,)),
-        dma((2, 8, 3)), dma((2, 8, 3)),
+        dma((3,)), dma((2, 2)), dma((2, 4, 3)), dma((2, 4, 3)),
         dma((2,)), dma((2,)), dma((2,)), dma((2,)),
         dma((2, 4, 2)), dma((2, 4, 2)), dma((2,)),
     ]

time: 114 us -> 111 us (0.974)
  Pallas kernels: 111 us -> 108 us
    pallas_call x1, Pallas kernels: 111 us -> 108 us  [per_device(): pl.pallas_call(kernel, out_shape=(jax.ShapeDtypeStruct((128, 512), BF16),...]
where the time goes in v6:
time: 111 us
  Pallas kernels  108 us (97%)
  local copies, waits for them, and re-layouts  2.19 us (2%)
    pallas_call x1, Pallas kernels, per_device(): pl.pallas_call(kernel, out_shape=(jax.ShapeDtypeStruct((128, 512), BF16),...  108 us

profile of v6, /device:TPU:1, one launch (start us, length us, event | category | flops | bytes accessed | tf_op | source)
XLA Modules:
  0.0 111.0 jit_solution(9748844784962826640)
XLA Ops:
  0.6 108.2 %shard_map.77 = (bf16[128,512]{1,0:T(8,128)(2,1)}, bf16[1,128,128]{2,1,0:T(8,128)(2,1)}) custom-call(bf16[128,512]{1,0:T(8,128)(2,1)} %q_in.1, bf16[128,512]{1,0:T(8,128)(2,1)} %k_in.1, bf16[128,512]{1,0:T(8,128)(2,1)} %v_in.1, bf16[128,512]{1,0:T(8,128)(2,1)} %x_in.1, bf16[8,32,512]{2,1,0:T(8,128)(2,1)} %bitcast.4, bf16[3,256,128]{2,1,0:T(8,128)(2,1)} %bitcast.5), custom_call_target="tpu_custom_call" | custom-call | tf_op jit(solution)/shard_map/pallas_call | solution.py:542
  108.8 0.0 copy-start
  108.8 1.6 %copy.10 = bf16[128,512]{1,0:T(8,128)(2,1)} copy(bf16[128,512]{1,0:T(8,128)(2,1)} %get-tuple-element.4) | data formatting | bytes 262144
  110.4 0.0 copy-done
  110.4 0.6 copy.11
Async XLA Ops:
  108.8 1.6 %copy-start = (bf16[1,128,128]{2,1,0:T(8,128)(2,1)S(1)}, bf16[1,128,128]{2,1,0:T(8,128)(2,1)}, u32[]{:S(2)}) copy-start(bf16[1,128,128]{2,1,0:T(8,128)(2,1)} %get-tuple-element.5) | copy-start | bytes 98308

commit v7 on v5

--- a/solution.py
+++ b/solution.py
@@ -166,9 +166,18 @@
     loop(0, 2, own_part)
     has_before = ctx > 0
 
+    def send_weights(j):
+        to = lax.rem(s + j, 8)
+        remote(cw_in.at[to], wt_v.at[core, s], ws.at[0], wr.at[0], (z * 8 + to, head))
+
+    def all_weights():
+        loop(1, 8, send_weights)
+        pltpu.make_async_copy(cw_in.at[s], wt_v.at[core, s], wr.at[0]).start()
+
     def whole_part(hp):
         whole_wait(pk_v.at[hp], fr.at[2 * hp])
         whole_wait(pv_v.at[hp], fr.at[2 * hp + 1])
+        pl.when(hp == 1)(all_weights)
         for j in range(2):
             i = 2 * hp + j
             cols = pl.ds(pl.multiple_of(i * 128, 128), 128)
@@ -204,9 +213,12 @@
 
         @pl.when(hp == 0)
         def _():
-            loop(0, 2, lambda m: weights_step(1, m))
-
-
+            loop(1, 3, lambda m: weights_step(1, m))
+
+        pl.when(hp == 1)(lambda: weights_step(2, 0))
+
+
+    weights_step(1, 0)
     loop(0, 2, whole_part)
 
     parts = [(hp, c) for hp in range(2) for c in range(2)]
@@ -241,14 +253,7 @@
             pass_right(1, hp, c)
             pass_left(1, hp, c)
 
-    def send_weights(j):
-        to = lax.rem(s + j, 8)
-        remote(cw_in.at[to], wt_v.at[core, s], ws.at[0], wr.at[0], (z * 8 + to, head))
-
-    loop(1, 8, send_weights)
-    pltpu.make_async_copy(cw_in.at[s], wt_v.at[core, s], wr.at[0]).start()
-    weights_step(1, 2)
-    loop(0, 3, lambda m: weights_step(2, m))
+    loop(1, 3, lambda m: weights_step(2, m))
     fo_cp = pltpu.make_async_copy(fo_v, fine_out, out_sem.at[0])
     fo_cp.start()
 
@@ -367,6 +372,8 @@
         ringing = pl.when(i < GROUPS)
         ringing(lambda: odd(parts[:2]))
 
+        ringing(lambda: odd(parts[2:]))
+
         @pl.when(i == 0)
         def _():
             whole_wait(wt_v.at[core], wr.at[0])
@@ -374,14 +381,13 @@
             pw_own.wait()
             acc_v[...] = jnp.zeros_like(acc_v)
 
-        ringing(lambda: odd(parts[2:]))
         weighing = pl.when(i < GROUPS - 1)
         weighing(lambda: weights_step(i + 3, 0))
-        pl.when(i == 0)(lambda: turn(core))
         pl.when((i >= 2) & (i < GROUPS + 2))(lambda: spread(i - 2))
         pl.when((i >= 1) & (i < GROUPS + 1))(lambda: reduce(i - 1))
         pl.when(i == GROUPS + 2)(weights_end)
         ringing(lambda: even(parts[:2]))
+        pl.when(i == 0)(lambda: turn(core))
         weighing(lambda: weights_step(i + 3, 1))
         ringing(lambda: even(parts[2:]))
         weighing(lambda: weights_step(i + 3, 2))

time: 107 us -> 106 us (level)
    pallas_call x1, Pallas kernels: 104 us -> 103 us  [per_device(): pl.pallas_call(kernel, out_shape=(jax.ShapeDtypeStruct((128, 512), BF16),...]
where the time goes in v7:
time: 106 us; the launch traced here: 105 us
  Pallas kernels  103 us (97%)
  local copies, waits for them, and re-layouts  2.19 us (2%)
    pallas_call x1, Pallas kernels, per_device(): pl.pallas_call(kernel, out_shape=(jax.ShapeDtypeStruct((128, 512), BF16),...  103 us
    unnamed x4, local copies, waits for them, and re-layouts  2.19 us

profile of v7, /device:TPU:1, one launch (start us, length us, event | category | flops | bytes accessed | tf_op | source)
XLA Modules:
  0.0 105.4 jit_solution(6637336508952904353)
XLA Ops:
  0.6 102.6 %shard_map.77 = (bf16[128,512]{1,0:T(8,128)(2,1)}, bf16[1,128,128]{2,1,0:T(8,128)(2,1)}) custom-call(bf16[128,512]{1,0:T(8,128)(2,1)} %q_in.1, bf16[128,512]{1,0:T(8,128)(2,1)} %k_in.1, bf16[128,512]{1,0:T(8,128)(2,1)} %v_in.1, bf16[128,512]{1,0:T(8,128)(2,1)} %x_in.1, bf16[8,32,512]{2,1,0:T(8,128)(2,1)} %bitcast.4, bf16[3,256,128]{2,1,0:T(8,128)(2,1)} %bitcast.5), custom_call_target="tpu_custom_call" | custom-call | tf_op jit(solution)/shard_map/pallas_call | solution.py:555
  103.2 0.0 copy-start
  103.2 1.6 %copy.10 = bf16[128,512]{1,0:T(8,128)(2,1)} copy(bf16[128,512]{1,0:T(8,128)(2,1)} %get-tuple-element.4) | data formatting | bytes 262144
  104.8 0.0 copy-done
  104.8 0.6 copy.11
Async XLA Ops:
  103.2 1.6 %copy-start = (bf16[1,128,128]{2,1,0:T(8,128)(2,1)S(1)}, bf16[1,128,128]{2,1,0:T(8,128)(2,1)}, u32[]{:S(2)}) copy-start(bf16[1,128,128]{2,1,0:T(8,128)(2,1)} %get-tuple-element.5) | copy-start | bytes 98308

commit v8 on v7

--- a/solution.py
+++ b/solution.py
@@ -14,7 +14,7 @@
 SCALE = HEAD_DIM ** -0.5
 NEG = -1e30
 GROUPS = 4
-ORDER = (1, 2, 0)
+ORDER = (1, 0, 2)
 
 
 def slot_of(offset):
@@ -177,7 +177,7 @@
     def whole_part(hp):
         whole_wait(pk_v.at[hp], fr.at[2 * hp])
         whole_wait(pv_v.at[hp], fr.at[2 * hp + 1])
-        pl.when(hp == 1)(all_weights)
+        pl.when(hp == 0)(all_weights)
         for j in range(2):
             i = 2 * hp + j
             cols = pl.ds(pl.multiple_of(i * 128, 128), 128)
@@ -317,7 +317,7 @@
             jnp.where(g == 3, 15, 2 * g + 2), jnp.where(g == 3, 14, 2 * g + 3),
         ]
 
-    def project(g):
+    def rows_of(g):
         slots = weight_slots(g)
         for slot in slots:
             for m in range(3):
@@ -329,13 +329,25 @@
             cc_v[slots[i]] = rows[:64]
             cc_v[slots[2 + i]] = rows[64:]
 
+    def sum_of(g, m):
+        terms = acc_v[m]
+        for slot in weight_slots(g):
+            terms = terms + dot(cc_v[slot], pw_v[slot, m])
+        return terms
+
+    def project(g):
+        rows_of(g)
+
         def one(m):
-            terms = acc_v[m]
-            for slot in slots:
-                terms = terms + dot(cc_v[slot], pw_v[slot, m])
-            acc_v[m] = terms
+            acc_v[m] = sum_of(g, m)
 
         loop(0, 3, one)
+
+    whole_wait(wt_v.at[core], wr.at[0])
+    remote(wt_v.at[core], wt_v.at[core], ws.at[2], wr.at[3], sibling)
+    pw_own.wait()
+    acc_v[...] = jnp.zeros_like(acc_v)
+    turn(core)
 
     def turn_of(i):
         more = i < GROUPS - 1
@@ -374,20 +386,11 @@
 
         ringing(lambda: odd(parts[2:]))
 
-        @pl.when(i == 0)
-        def _():
-            whole_wait(wt_v.at[core], wr.at[0])
-            remote(wt_v.at[core], wt_v.at[core], ws.at[2], wr.at[3], sibling)
-            pw_own.wait()
-            acc_v[...] = jnp.zeros_like(acc_v)
-
-        weighing = pl.when(i < GROUPS - 1)
+        weighing = ringing
         weighing(lambda: weights_step(i + 3, 0))
         pl.when((i >= 2) & (i < GROUPS + 2))(lambda: spread(i - 2))
         pl.when((i >= 1) & (i < GROUPS + 1))(lambda: reduce(i - 1))
-        pl.when(i == GROUPS + 2)(weights_end)
         ringing(lambda: even(parts[:2]))
-        pl.when(i == 0)(lambda: turn(core))
         weighing(lambda: weights_step(i + 3, 1))
         ringing(lambda: even(parts[2:]))
         weighing(lambda: weights_step(i + 3, 2))
@@ -399,13 +402,15 @@
 
         ringing(lambda: conv(i))
 
-        @pl.when((i == GROUPS - 1) | (i == GROUPS))
-        def _():
-            loop(0, 3, lambda m: weights_step(i + 3, m))
+        @pl.when(i == GROUPS)
+        def _():
+            loop(0, 3, lambda m: weights_step(7, m))
 
         pl.when(i >= 3)(lambda: project(i - 3))
 
-    loop(0, GROUPS + 3, turn_of)
+    loop(0, GROUPS + 2, turn_of)
+    weights_end()
+    rows_of(GROUPS - 1)
 
     first = core == 0
 
@@ -420,10 +425,9 @@
 
     offset = lax.rem(chip - z + NZ, NZ)
     place = jnp.where(offset == 0, 0, jnp.where(offset <= 8, 7 + offset, NZ - offset))
-    send_back(1, cc_v[place])
     kv_cp = []
     for m in ORDER:
-        both = acc_v[m].astype(BF16)
+        both = sum_of(GROUPS - 1, m).astype(BF16)
         if m == 0:
             send_back(0, both)
             continue
@@ -441,6 +445,8 @@
         kv_cp.append(
             remote(ys_v.at[i, 1 - core], kv_v.at[i, 1, core], ks.at[i, 1, 0], kr.at[i, 1, core], sibling)
         )
+    send_back(1, cc_v[place])
+
     for i in range(4):
         whole_wait(pk_v.at[0], fs.at[i])
     whole_wait(wt_v.at[0, pl.ds(0, 7)], ws.at[0])
@@ -479,19 +485,17 @@
     for m in range(3):
         whole_wait(held(0, m), wzs.at[0 if m == 2 else 1, 7, m])
     loop(0, NZ, lambda k: [whole_wait(held(0, m), wss.at[k, m]) for m in range(3)])
-    for i in range(2):
-        for c in range(2):
-            whole_wait(f_v.at[i, c], xr.at[i, c])
-    for cp in swaps:
-        cp.wait_send()
-    for i in range(2):
+    def keys_here(i):
         whole_wait(kv_v.at[i, 1, 1 - core], kr.at[i, 1, 1 - core])
         for back in (0, 2, 3):
             for c in range(2):
                 whole_wait(kv_v.at[i, back, c], kr.at[i, back, c])
-
+        for c in range(2):
+            whole_wait(f_v.at[i, c], xr.at[i, c])
+
+    keys_here(0)
     q = f_v[0].reshape(128, 128)
-    keys, vals = [[kv_v[i, back].reshape(128, 128) for back in range(4)] for i in range(2)]
+    keys = [kv_v[0, back].reshape(128, 128) for back in range(4)]
     scores = []
     for back in range(4):
         seen = causal if back == 0 else z >= back
@@ -499,19 +503,15 @@
     top = scores[0].max(1, keepdims=True)
     for back in range(1, 4):
         top = jnp.maximum(top, scores[back].max(1, keepdims=True))
-    total = None
-    mixed = None
-    for back in range(4):
-        e = jnp.exp(scores[back] - top)
-        part_sum = jnp.sum(e, 1, keepdims=True)
-        part_mix = dot(e.astype(BF16), vals[back])
-        total = part_sum if total is None else total + part_sum
-        mixed = part_mix if mixed is None else mixed + part_mix
+    weights = [jnp.exp(scores[back] - top) for back in range(4)]
+    total = sum(jnp.sum(e, 1, keepdims=True) for e in weights)
+    keys_here(1)
+    mixed = sum(dot(weights[back].astype(BF16), kv_v[1, back].reshape(128, 128)) for back in range(4))
     co_v[...] = (f_v[1].reshape(128, 128).astype(F32) + mixed / total).astype(BF16)
     co_cp = pltpu.make_async_copy(co_v, coarse_out.at[0], out_sem.at[1])
     co_cp.start()
 
-    for cp in kv_cp:
+    for cp in swaps + kv_cp:
         cp.wait_send()
     fo_cp.wait()
     co_cp.wait()

time: 106 us -> 105 us (level)
  no operation moved by 1% of the time
where the time goes in v8:
time: 105 us
  Pallas kernels  102 us (97%)
  local copies, waits for them, and re-layouts  2.19 us (2%)
    pallas_call x1, Pallas kernels, per_device(): pl.pallas_call(kernel, out_shape=(jax.ShapeDtypeStruct((128, 512), BF16),...  102 us
    unnamed x4, local copies, waits for them, and re-layouts  2.19 us

profile of v8, /device:TPU:1, one launch (start us, length us, event | category | flops | bytes accessed | tf_op | source)
XLA Modules:
  0.0 105.3 jit_solution(5130822417376085903)
XLA Ops:
  0.6 102.5 %shard_map.77 = (bf16[128,512]{1,0:T(8,128)(2,1)}, bf16[1,128,128]{2,1,0:T(8,128)(2,1)}) custom-call(bf16[128,512]{1,0:T(8,128)(2,1)} %q_in.1, bf16[128,512]{1,0:T(8,128)(2,1)} %k_in.1, bf16[128,512]{1,0:T(8,128)(2,1)} %v_in.1, bf16[128,512]{1,0:T(8,128)(2,1)} %x_in.1, bf16[8,32,512]{2,1,0:T(8,128)(2,1)} %bitcast.4, bf16[3,256,128]{2,1,0:T(8,128)(2,1)} %bitcast.5), custom_call_target="tpu_custom_call" | custom-call | tf_op jit(solution)/shard_map/pallas_call | solution.py:555
  103.1 0.0 copy-start
  103.1 1.6 %copy.10 = bf16[128,512]{1,0:T(8,128)(2,1)} copy(bf16[128,512]{1,0:T(8,128)(2,1)} %get-tuple-element.4) | data formatting | bytes 262144
  104.7 0.0 copy-done
  104.7 0.6 copy.11
Async XLA Ops:
  103.1 1.6 %copy-start = (bf16[1,128,128]{2,1,0:T(8,128)(2,1)S(1)}, bf16[1,128,128]{2,1,0:T(8,128)(2,1)}, u32[]{:S(2)}) copy-start(bf16[1,128,128]{2,1,0:T(8,128)(2,1)} %get-tuple-element.5) | copy-start | bytes 98308

commit v9 on v8

--- a/solution.py
+++ b/solution.py
@@ -222,6 +222,7 @@
     loop(0, 2, whole_part)
 
     parts = [(hp, c) for hp in range(2) for c in range(2)]
+    ring_parts = [(0, 0), (1, 0)]
 
     def place_right(k):
         return jnp.where(k == 8, 15, k)
@@ -231,27 +232,26 @@
 
     def pass_right(k, hp, c):
         remote(
-            acts.at[place_right(k - 1), hp, c], acts.at[place_right(k), hp, c],
+            acts.at[place_right(k - 1), hp], acts.at[place_right(k), hp],
             zs.at[0, k - 1, hp, c], zr.at[0, k - 1, hp, c], right,
         )
 
     def pass_left(k, hp, c):
         remote(
-            acts.at[place_left(k - 1), hp, c], acts.at[place_left(k), hp, c],
+            acts.at[place_left(k - 1), hp], acts.at[place_left(k), hp],
             zs.at[1, k - 1, hp, c], zr.at[1, k - 1, hp, c], left,
         )
 
     def got_right(k, hp, c):
-        whole_wait(acts.at[place_right(k), hp, c], zr.at[0, k - 1, hp, c])
+        whole_wait(acts.at[place_right(k), hp], zr.at[0, k - 1, hp, c])
 
     def got_left(k, hp, c):
-        whole_wait(acts.at[place_left(k), hp, c], zr.at[1, k - 1, hp, c])
+        whole_wait(acts.at[place_left(k), hp], zr.at[1, k - 1, hp, c])
 
     for hp in range(2):
         whole_wait(acts.at[0, hp], ar.at[hp])
-        for c in range(2):
-            pass_right(1, hp, c)
-            pass_left(1, hp, c)
+        pass_right(1, hp, 0)
+        pass_left(1, hp, 0)
 
     loop(1, 3, lambda m: weights_step(2, m))
     fo_cp = pltpu.make_async_copy(fo_v, fine_out, out_sem.at[0])
@@ -382,17 +382,17 @@
                     pass_left(k + 1, hp, c)
 
         ringing = pl.when(i < GROUPS)
-        ringing(lambda: odd(parts[:2]))
-
-        ringing(lambda: odd(parts[2:]))
+        ringing(lambda: odd(ring_parts[:1]))
+
+        ringing(lambda: odd(ring_parts[1:]))
 
         weighing = ringing
         weighing(lambda: weights_step(i + 3, 0))
         pl.when((i >= 2) & (i < GROUPS + 2))(lambda: spread(i - 2))
         pl.when((i >= 1) & (i < GROUPS + 1))(lambda: reduce(i - 1))
-        ringing(lambda: even(parts[:2]))
+        ringing(lambda: even(ring_parts[:1]))
         weighing(lambda: weights_step(i + 3, 1))
-        ringing(lambda: even(parts[2:]))
+        ringing(lambda: even(ring_parts[1:]))
         weighing(lambda: weights_step(i + 3, 2))
 
         @pl.when(i == 0)
@@ -460,10 +460,9 @@
             whole_wait(ts_v.at[hp, 0], as_.at[2 + hp])
 
     def ring_left(k):
-        for c in range(2):
-            for way in range(2):
-                whole_wait(acts.at[0, 0, c], zs.at[way, k, way, c])
-                pl.when(k < 7)(lambda: whole_wait(acts.at[0, 0, c], zs.at[way, k, 1 - way, c]))
+        for way in range(2):
+            whole_wait(acts.at[0, 0], zs.at[way, k, way, 0])
+            pl.when(k < 7)(lambda: whole_wait(acts.at[0, 0], zs.at[way, k, 1 - way, 0]))
 
     loop(0, 8, ring_left)
     loop(0, GROUPS, lambda g: whole_wait(sb_v.at[g, pl.ds(0, 15)], ss.at[g]))

time: 105 us -> 106 us (level)
  no operation moved by 1% of the time
where the time goes in v9:
time: 106 us
  Pallas kernels  103 us (97%)
  local copies, waits for them, and re-layouts  2.19 us (2%)
    pallas_call x1, Pallas kernels, per_device(): pl.pallas_call(kernel, out_shape=(jax.ShapeDtypeStruct((128, 512), BF16),...  103 us
    unnamed x4, local copies, waits for them, and re-layouts  2.19 us

profile of v9, /device:TPU:1, one launch (start us, length us, event | category | flops | bytes accessed | tf_op | source)
XLA Modules:
  0.0 105.6 jit_solution(5528637189009308783)
XLA Ops:
  0.6 102.7 %shard_map.77 = (bf16[128,512]{1,0:T(8,128)(2,1)}, bf16[1,128,128]{2,1,0:T(8,128)(2,1)}) custom-call(bf16[128,512]{1,0:T(8,128)(2,1)} %q_in.1, bf16[128,512]{1,0:T(8,128)(2,1)} %k_in.1, bf16[128,512]{1,0:T(8,128)(2,1)} %v_in.1, bf16[128,512]{1,0:T(8,128)(2,1)} %x_in.1, bf16[8,32,512]{2,1,0:T(8,128)(2,1)} %bitcast.4, bf16[3,256,128]{2,1,0:T(8,128)(2,1)} %bitcast.5), custom_call_target="tpu_custom_call" | custom-call | tf_op jit(solution)/shard_map/pallas_call | solution.py:554
  103.4 0.0 copy-start
  103.4 1.6 %copy.10 = bf16[128,512]{1,0:T(8,128)(2,1)} copy(bf16[128,512]{1,0:T(8,128)(2,1)} %get-tuple-element.4) | data formatting | bytes 262144
  105.0 0.0 copy-done
  105.0 0.6 copy.11
Async XLA Ops:
  103.4 1.6 %copy-start = (bf16[1,128,128]{2,1,0:T(8,128)(2,1)S(1)}, bf16[1,128,128]{2,1,0:T(8,128)(2,1)}, u32[]{:S(2)}) copy-start(bf16[1,128,128]{2,1,0:T(8,128)(2,1)} %get-tuple-element.5) | copy-start | bytes 98308

commit v10 on v8

--- a/solution.py
+++ b/solution.py
@@ -110,13 +110,15 @@
     def held(slot, m):
         return pw_v.at[slot, m, :, lanes]
 
+    def whole(slot):
+        return pw_v.at[slot, :, :, lanes]
+
     pw_own = pltpu.make_async_copy(pw_in, pw_v.at[0, :, :, lanes], wr.at[2])
     pw_own.start()
     for m in range(3):
         remote(pw_in.at[m], held(1, m), wzs.at[0, 0, m], wzr.at[0, 0, m], right)
         remote(pw_in.at[m], held(8, m), wzs.at[1, 0, m], wzr.at[1, 0, m], left)
-    for m in range(3):
-        remote(pw_in.at[m], held(0, m), wss.at[0, m], wsr.at[0, m], sibling)
+    remote(pw_in, whole(0), wss.at[0, 0], wsr.at[0, 0], sibling)
 
     def weights_step(k, m):
         whole_wait(held(k, m), wzr.at[0, k - 1, m])
@@ -138,13 +140,16 @@
         def _():
             remote(held(14, m), held(15, m), wss.at[15, m], wsr.at[15, m], plane_at(NZ - 1, 1 - core))
 
-        remote(held(k, m), held(k, m), wss.at[k, m], wsr.at[k, m], sibling)
-        remote(held(7 + k, m), held(7 + k, m), wss.at[7 + k, m], wsr.at[7 + k, m], sibling)
+        @pl.when(m == 2)
+        def _():
+            for slot in (k, 7 + k):
+                remote(whole(slot), whole(slot), wss.at[slot, 0], wsr.at[slot, 0], sibling)
 
     def weights_end():
         for m in range(3):
             way = 0 if m == 2 else 1
             whole_wait(held(15, m), wzr.at[way, 7, m])
+            whole_wait(pw_v.at[15, m, :, other_lanes], wsr.at[15, m])
 
     row = lax.broadcasted_iota(jnp.int32, (128, 128), 0)
     col = lax.broadcasted_iota(jnp.int32, (128, 128), 1)
@@ -320,8 +325,7 @@
     def rows_of(g):
         slots = weight_slots(g)
         for slot in slots:
-            for m in range(3):
-                whole_wait(pw_v.at[slot, m, :, other_lanes], wsr.at[slot, m])
+            pl.when(slot != 15)(lambda: whole_wait(pw_v.at[slot, :, :, other_lanes], wsr.at[slot, 0]))
         whole_wait(gb_v.at[g], gr.at[g])
         for i in range(2):
             got = gb_v[g, :, i].astype(F32)
@@ -484,7 +488,10 @@
     loop(0, 7, weights_left)
     for m in range(3):
         whole_wait(held(0, m), wzs.at[0 if m == 2 else 1, 7, m])
-    loop(0, NZ, lambda k: [whole_wait(held(0, m), wss.at[k, m]) for m in range(3)])
+    loop(0, NZ - 1, lambda k: whole_wait(whole(0), wss.at[k, 0]))
+    for m in range(3):
+        whole_wait(held(0, m), wss.at[15, m])
+
     def keys_here(i):
         whole_wait(kv_v.at[i, 1, 1 - core], kr.at[i, 1, 1 - core])
         for back in (0, 2, 3):

time: 105 us -> 105 us (level)
  no operation moved by 1% of the time
where the time goes in v10:
time: 105 us
  Pallas kernels  102 us (97%)
  local copies, waits for them, and re-layouts  2.19 us (2%)
    pallas_call x1, Pallas kernels, per_device(): pl.pallas_call(kernel, out_shape=(jax.ShapeDtypeStruct((128, 512), BF16),...  102 us
    unnamed x4, local copies, waits for them, and re-layouts  2.19 us

profile of v10, /device:TPU:1, one launch (start us, length us, event | category | flops | bytes accessed | tf_op | source)
XLA Modules:
  0.0 105.3 jit_solution(18410592047518912875)
XLA Ops:
  0.6 102.5 %shard_map.77 = (bf16[128,512]{1,0:T(8,128)(2,1)}, bf16[1,128,128]{2,1,0:T(8,128)(2,1)}) custom-call(bf16[128,512]{1,0:T(8,128)(2,1)} %q_in.1, bf16[128,512]{1,0:T(8,128)(2,1)} %k_in.1, bf16[128,512]{1,0:T(8,128)(2,1)} %v_in.1, bf16[128,512]{1,0:T(8,128)(2,1)} %x_in.1, bf16[8,32,512]{2,1,0:T(8,128)(2,1)} %bitcast.4, bf16[3,256,128]{2,1,0:T(8,128)(2,1)} %bitcast.5), custom_call_target="tpu_custom_call" | custom-call | tf_op jit(solution)/shard_map/pallas_call | solution.py:562
  103.1 0.0 copy-start
  103.1 1.6 %copy.10 = bf16[128,512]{1,0:T(8,128)(2,1)} copy(bf16[128,512]{1,0:T(8,128)(2,1)} %get-tuple-element.4) | data formatting | bytes 262144
  104.7 0.0 copy-done
  104.7 0.6 copy.11
Async XLA Ops:
  103.1 1.6 %copy-start = (bf16[1,128,128]{2,1,0:T(8,128)(2,1)S(1)}, bf16[1,128,128]{2,1,0:T(8,128)(2,1)}, u32[]{:S(2)}) copy-start(bf16[1,128,128]{2,1,0:T(8,128)(2,1)} %get-tuple-element.5) | copy-start | bytes 98308
